TPU v7x, 128 devices: a whole 4x4x4 slice. The times are simulated.
128 devices in a mesh: rep: 8 (over y, core), sp: 16 (over x, z).
Axes of the slice: x: 4, y: 4, z: 4, core: 2. Of those that a mesh axis runs over, the one named last changes fastest.
Arguments:
- frames: bfloat16 [8, 64, 256, 1024], P('rep', 'sp'), may hold values from -6 to 6
- out_grad: bfloat16 [8, 64, 256, 1024], P('rep', 'sp'), may hold values from -0.046875 to 0.046875
- error_prev: float32 [8, 9216, 1024], P('rep', 'sp'), may hold values from -6 to 6
- q_prev: float32 [32, 9216], P(None, 'sp'), may hold values from -6 to 6
Outputs:
- error_next: float32 [8, 9216, 1024], P('rep', 'sp')
- q_next: float32 [32, 9216], P(None, 'sp')
All inputs are finite; a program needn't handle non-finite values.
Results may differ from a plain program's by a relative error of at most 0.0003.
Values may be sent and summed in bfloat16 or wider, within the bound.
A program may use at most 192 MiB of HBM per device.

v0:
```python
import jax
import jax.numpy as jnp
from jax import lax
from jax.sharding import PartitionSpec as P


def with_halo(block, sides, width):
    for axis, dim in sides:
        count = lax.axis_size(axis)
        forward = [(i, i + 1) for i in range(count - 1)]
        backward = [(target, source) for source, target in forward]
        low = lax.ppermute(
            lax.slice_in_dim(block, block.shape[dim] - width, None, axis=dim), axis, forward
        )
        high = lax.ppermute(lax.slice_in_dim(block, 0, width, axis=dim), axis, backward)
        block = jnp.concatenate([low, block, high], axis=dim)
    return block


def make_patches(padded, top, count, width):
    taps = []
    for row_off in range(3):
        block = lax.dynamic_slice_in_dim(padded, top + row_off, count, 0)
        for col_off in range(3):
            taps.append(block[:, col_off : col_off + width, :])
    stacked = jnp.stack(taps, axis=-1)
    return stacked.reshape(count * width, stacked.shape[2] * 9)


def per_device(frames, out_grad, error_prev, q_prev):
    high = lax.Precision.HIGHEST
    band_rows = frames.shape[1]
    width = frames.shape[2]
    chans = frames.shape[3]
    extended = with_halo(frames, (("sp", 1),), 1)
    padded = jnp.pad(extended[0], ((0, 0), (1, 1), (0, 0)))
    flat_grad = out_grad[0].reshape(band_rows * width, chans)
    cols = make_patches(padded, 0, band_rows, width)
    grad_rows = lax.psum_scatter(
        lax.dot_general(
            cols, flat_grad, (((0,), (0,)), ((), ())), preferred_element_type=jnp.float32
        ),
        "sp",
        scatter_dimension=0,
        tiled=True,
    )
    memory = grad_rows + error_prev[0]
    p_term = jnp.dot(q_prev, memory, precision=high)
    p_total = lax.psum(lax.psum(p_term, "sp"), "rep")
    gram = jnp.dot(p_total, p_total.T, precision=high)
    lower = jnp.linalg.cholesky(gram)
    p_ortho = jax.scipy.linalg.solve_triangular(lower, p_total, lower=True)
    q_term = lax.dot_general(p_ortho, memory, (((1,), (1,)), ((), ())), precision=high)
    q_next = lax.psum(q_term, "rep") / lax.axis_size("rep")
    approx = lax.dot_general(q_next, p_ortho, (((0,), (0,)), ((), ())), precision=high)
    error_next = memory - approx
    return (error_next[None], q_next)


def solution(mesh):
    placed = (
        P("rep", "sp", None, None),
        P("rep", "sp", None, None),
        P("rep", "sp", None),
        P(None, "sp"),
    )
    return jax.shard_map(
        per_device,
        mesh=mesh,
        in_specs=placed,
        out_specs=(P("rep", "sp", None), P(None, "sp")),
        check_vma=False,
    )
```

profile of v0, /device:TPU:1, one launch (start us, length us, event | category | flops | bytes accessed | tf_op | source)
XLA Modules:
  0.0 571.6 jit_solution(5684949523990615980)
XLA Ops:
  7.2 0.0 copy-start
  7.2 0.0 reduce-scatter.2.cloned.1.call-start
  7.2 0.0 copy-start.2
  7.2 1.4 fusion.9
  8.7 4.5 collective-permute-start
  13.2 1.3 collective-permute-start.1
  14.5 9.2 %collective-permute-done = bf16[1,1,256,1024]{3,2,1,0:T(8,128)(2,1)S(1)} collective-permute-done((bf16[1,1,256,1024]{3,2,1,0:T(8,128)(2,1)S(1)}, bf16[1,1,256,1024]{3,2,1,0:T(8,128)(2,1)S(1)}, u32[]{:S(2)}, u32[]{:S(2)}) %collective-permute-start) | collective-permute-done | bytes 524320 | tf_op jit(solution)/shard_map/ppermute | solution.py:12
  23.7 4.2 collective-permute-done.1
  27.9 0.0 copy-done.2
  27.9 0.4 maximum_bitcast_fusion
  28.3 1.9 bitcast_dynamic-update-slice_fusion.6
  30.2 1.5 fusion.3
  31.7 1.9 bitcast_dynamic-update-slice_fusion.5
  33.6 2.0 bitcast_dynamic-update-slice_fusion.4
  35.6 1.5 bitcast_dynamic-update-slice_fusion.3
  37.0 1.9 bitcast_dynamic-update-slice_fusion.2
  38.9 1.9 bitcast_dynamic-update-slice_fusion.1
  40.8 1.5 fusion.1
  42.3 1.9 bitcast_dynamic-update-slice_fusion
  44.3 29.2 %copy.7 = bf16[4,256,1024,9]{1,0,3,2:T(4,128)(2,1)} copy(bf16[4,256,1024,9]{2,1,0,3:T(8,128)(2,1)} %bitcast_dynamic-update-slice_fusion) | data formatting | bytes 37748736 | tf_op jit(solution)/shard_map/stack | solution.py:26
  73.5 19.9 %copy.9 = bf16[1152,8,4,256]{3,1,2,0:T(8,128)(2,1)} copy(bf16[1152,8,4,256]{3,2,1,0:T(4,128)(2,1)} %bitcast.59) | data formatting | bytes 37748736
  93.3 0.0 copy-done
  93.3 28.1 %fusion.10 = f32[9216,1024]{1,0:T(8,128)} fusion(bf16[1024,9216]{0,1:T(8,128)(2,1)} %bitcast.60, bf16[1024,1024]{1,0:T(8,128)(2,1)S(1)} %bitcast.58), kind=kOutput, calls=%fused_computation.30 | convolution fusion | flops 19327352832 | bytes 58720256 | tf_op jit(solution)/shard_map/dot_general | solution.py:40
  121.4 0.0 copy-start.4
  121.4 0.0 reduce-scatter.2.cloned.1.call-update
  121.4 0.0 all-reduce.5.cloned.1.call-start
  121.5 219.7 %reduce-scatter.2.cloned.1.call-done = f32[576,1024]{1,0:T(8,128)} async-done(((f32[9216,1024]{1,0:T(8,128)}), f32[576,1024]{1,0:T(8,128)}) %reduce-scatter.2.cloned.1.call-update) | async-done | bytes 2359312 | tf_op jit(solution)/shard_map/reduce_scatter | solution.py:39
  341.2 0.0 copy-done.4
  341.2 4.6 convolution_bitcast_fusion
  345.8 0.0 all-reduce.5.cloned.1.call-update
  345.9 0.0 all-reduce.7.cloned.1.call-start
  345.9 80.6 %all-reduce.5.cloned.1.call-done = f32[32,1024]{1,0:T(8,128)} async-done(((f32[32,1024]{1,0:T(8,128)}), f32[32,1024]{1,0:T(8,128)}) %all-reduce.5.cloned.1.call-update) | async-done | bytes 131088 | tf_op jit(solution)/shard_map/psum | solution.py:49
  426.5 0.0 all-reduce.7.cloned.1.call-update
  426.6 0.3 all-reduce.9.cloned.1.call-start
  426.8 60.1 %all-reduce.7.cloned.1.call-done = f32[32,1024]{1,0:T(8,128)} async-done(((f32[32,1024]{1,0:T(8,128)}), f32[32,1024]{1,0:T(8,128)}) %all-reduce.7.cloned.1.call-update) | async-done | bytes 131088 | tf_op jit(solution)/shard_map/psum | solution.py:49
  487.0 1.2 fusion.11
  488.2 0.1 copy.8
  488.3 2.9 cholesky.16
  491.3 0.6 compare_reduce_fusion
  491.9 0.7 fusion.4
  492.6 2.4 custom-call.7
  495.0 1.2 fusion.5
  496.2 5.1 fusion.8
  501.3 0.0 all-reduce.9.cloned.1.call-update
  501.3 56.8 %all-reduce.9.cloned.1.call-done = f32[32,576]{1,0:T(8,128)} async-done(((f32[32,576]{1,0:T(8,128)}), f32[32,576]{1,0:T(8,128)}) %all-reduce.9.cloned.1.call-update) | async-done | bytes 73744 | tf_op jit(solution)/shard_map/psum | solution.py:54
  558.1 0.0 copy-start.1
  558.1 1.0 broadcast_multiply_fusion
  559.1 0.0 copy-start.3
  559.2 6.0 %subtract_bitcast_fusion = f32[1,576,1024]{2,1,0:T(8,128)} fusion(f32[32,576]{1,0:T(8,128)S(1)} %broadcast_multiply_fusion, f32[32,1024]{1,0:T(8,128)S(1)} %fusion.5, f32[576,1024]{1,0:T(8,128)} %reduce-scatter.2.cloned.1.call-done, f32[1,576,1024]{2,1,0:T(8,128)} %param.6), kind=kOutput, calls=%fused_computation.2 | convolution fusion | flops 227672064 | bytes 7282688 | tf_op jit(solution)/shard_map/dot_general | solution.py:55
  565.1 0.0 copy-done.3
  565.1 0.0 copy-done.1
  (2 shorter events, 0.0 us)
Async XLA Ops:
  7.2 86.2 %copy-start = (bf16[1,4,256,1024]{3,2,1,0:T(8,128)(2,1)S(1)}, bf16[1,4,256,1024]{3,2,1,0:T(8,128)(2,1)}, u32[]{:S(2)}) copy-start(bf16[1,4,256,1024]{3,2,1,0:T(8,128)(2,1)} %param.5) | copy-start | bytes 6291460
  7.2 334.0 %reduce-scatter.2.cloned.1.call-start = ((), (), s32[]{:S(2)}) async-start(), calls=%async_computation.1 | async-start | bytes 40108032 | tf_op jit(solution)/shard_map/reduce_scatter | solution.py:39
  7.2 20.7 %copy-start.2 = (bf16[1,4,256,1024]{3,2,1,0:T(8,128)(2,1)S(1)}, bf16[1,4,256,1024]{3,2,1,0:T(8,128)(2,1)}, u32[]{:S(2)}) copy-start(bf16[1,4,256,1024]{3,2,1,0:T(8,128)(2,1)} %param.4) | copy-start | bytes 6291460
  8.7 15.1 %collective-permute-start = (bf16[1,1,256,1024]{3,2,1,0:T(8,128)(2,1)S(1)}, bf16[1,1,256,1024]{3,2,1,0:T(8,128)(2,1)S(1)}, u32[]{:S(2)}, u32[]{:S(2)}) collective-permute-start(bf16[1,1,256,1024]{3,2,1,0:T(8,128)(2,1)S(1)} %get-tuple-element.2), channel_id=1, source_target_pairs={{0,1},{1,2},{2,3},{3,4},{4,5},{5,6},{6,7},{7,8},{8,9},{9,10},{10,1... | collective-permute-start | bytes 1572872 | tf_op jit(solution)/shard_map/ppermute | solution.py:12
  13.2 14.7 %collective-permute-start.1 = (bf16[1,1,256,1024]{3,2,1,0:T(8,128)(2,1)S(1)}, bf16[1,1,256,1024]{3,2,1,0:T(8,128)(2,1)S(1)}, u32[]{:S(2)}, u32[]{:S(2)}) collective-permute-start(bf16[1,1,256,1024]{3,2,1,0:T(8,128)(2,1)S(1)} %get-tuple-element.3), channel_id=1, source_target_pairs={{1,0},{2,1},{3,2},{4,3},{5,4},{6,5},{7,6},{8,7},{9,8},{10,9},{11,1... | collective-permute-start | bytes 1572872 | tf_op jit(solution)/shard_map/ppermute | solution.py:15
  121.4 219.8 %copy-start.4 = (f32[32,576]{1,0:T(8,128)S(1)}, f32[32,576]{1,0:T(8,128)}, u32[]{:S(2)}) copy-start(f32[32,576]{1,0:T(8,128)} %param.7) | copy-start | bytes 221188
  121.4 305.1 %all-reduce.5.cloned.1.call-start = ((), (), s32[]{:S(2)}) async-start(), calls=%async_computation.2 | async-start | bytes 262144 | tf_op jit(solution)/shard_map/psum | solution.py:49
  345.9 141.1 %all-reduce.7.cloned.1.call-start = ((), (), s32[]{:S(2)}) async-start(), calls=%async_computation.3 | async-start | bytes 262144 | tf_op jit(solution)/shard_map/psum | solution.py:49
  426.6 131.5 %all-reduce.9.cloned.1.call-start = ((), (), s32[]{:S(2)}) async-start(), calls=%async_computation.4 | async-start | bytes 163840 | tf_op jit(solution)/shard_map/psum | solution.py:54
  558.1 7.0 %copy-start.1 = (bf16[1,4,256,1024]{3,2,1,0:T(8,128)(2,1)S(1)}, bf16[1,4,256,1024]{3,2,1,0:T(8,128)(2,1)}, u32[]{:S(2)}) copy-start(bf16[1,4,256,1024]{3,2,1,0:T(8,128)(2,1)} %param.5) | copy-start | bytes 6291460
  559.1 6.0 %copy-start.3 = (f32[32,576]{1,0:T(8,128)}, f32[32,576]{1,0:T(8,128)S(1)}, u32[]{:S(2)}) copy-start(f32[32,576]{1,0:T(8,128)S(1)} %broadcast_multiply_fusion) | copy-start | bytes 221188
Sparse Core Ops, SparseCore 0:
  121.5 219.6 reduce-scatter.1
  346.0 80.5 all-reduce.4
  429.0 57.9 all-reduce.6
  501.5 56.5 all-reduce.8
where the time goes:
time: 573 us; the launch traced here: 572 us
  waiting for transfers between devices  431 us (75%)
  local copies, waits for them, and re-layouts  63.6 us (11%)
  matrix products  46.2 us (8%)
  between operations  13.8 us (2%)
  other arithmetic  11.1 us (2%)
  starting transfers between devices  6.21 us (1%)
    reduce_scatter x1, waiting for transfers between devices, per_device(): lax.psum_scatter(lax.dot_general(cols, flat_grad, (((0,), (0,)), ((), ())...  220 us
    psum x2, waiting for transfers between devices, per_device(): p_total = lax.psum(lax.psum(p_term, 'sp'), 'rep')  141 us
    psum x1, waiting for transfers between devices, per_device(): q_next = lax.psum(q_term, 'rep') / lax.axis_size('rep')  56.8 us
    another operation x2, local copies, waits for them, and re-layouts, make_patches(): stacked = jnp.stack(taps, axis=-1)  31.1 us
    unnamed x17, local copies, waits for them, and re-layouts  31 us
    dot_general x1, matrix products, per_device(): lax.dot_general(cols, flat_grad, (((0,), (0,)), ((), ())), preferred_elem...  28.1 us
  transfers between devices with their start and end apart: 6, of which 6 were waited for; matrix products, arithmetic and copies ran while one was open for 0% of the time, Pallas kernels for 0%

commit v1 on v0

v1 whole, which is shorter than its diff:
```python
import functools

import jax
import jax.numpy as jnp
from jax import lax
from jax.experimental import pallas as pl
from jax.experimental.pallas import tpu as pltpu
from jax.sharding import PartitionSpec as P

MESH = pl.DeviceIdType.MESH
RING = 4
CHUNKS = 8
COLS = 128
TAPS = 9
P_AT = 1


def sp_at(x, z):
    return {"sp": lax.rem(x + RING, RING) * RING + lax.rem(z + RING, RING)}


def remote(src, dst, send, recv, device):
    return pltpu.make_async_remote_copy(
        src_ref=src, dst_ref=dst, send_sem=send, recv_sem=recv, device_id=device, device_id_type=MESH
    )


def split(value):
    high = value.astype(jnp.bfloat16)
    rest = value - high.astype(jnp.float32)
    middle = rest.astype(jnp.bfloat16)
    low = (rest - middle.astype(jnp.float32)).astype(jnp.bfloat16)
    return high, middle, low


def exact_dot(a, b, contract):
    return lax.dot_general(
        a, b, (contract, ((), ())), precision=lax.Precision.HIGHEST, preferred_element_type=jnp.float32
    )


def step_kernel(
    count_rep, frames, g, err, q_own, q_taps, error_next, q_next,
    local, flipped, raw, halo, taps, gbuf, part, relay, piece, total,
    q_near, q_flip, t_term, t_near, p_src, p_near, p_one, p_far, p_all, p_ortho, work, q_src, q_got, q_sum, q_flat,
    l_in, f_send, f_recv, f_own, h_send, h_recv, e_in, g_own,
    d_send, d_recv, r_send, r_recv, a_send, a_recv, b_send, b_recv, out_sem,
    q_send, q_recv, q_copy, t_send, t_recv, s1, r1, s2, r2, s3, r3, s4, r4, s5, r5,
):
    sp, rep = lax.axis_index("sp"), lax.axis_index("rep")
    x, z = sp // RING, lax.rem(sp, RING)
    up, down = sp_at(x, z + 1), sp_at(x, z - 1)
    right, left = sp_at(x + 1, z), sp_at(x - 1, z)
    z_up, z_down = lax.rem(z + 1, RING), lax.rem(z + 3, RING)
    x_right, x_left, x_far = lax.rem(x + 1, RING), lax.rem(x + 3, RING), lax.rem(x + 2, RING)
    band = g.shape[0]
    half = band // 2
    count_sp = RING * RING
    share = part.shape[4] * 2
    width = halo.shape[3]
    rank = q_own.shape[0]

    def at_sp(d):
        return {"sp": lax.rem(sp + d, count_sp)}

    def at_rep(d):
        return {"rep": lax.rem(rep + d, count_rep)}

    def frames_out(step):
        return remote(
            flipped.at[:, lax.rem(z + step, RING)], raw.at[z], f_send.at[step - 1], f_recv.at[step - 1],
            sp_at(x, z + step),
        )

    def frames_in(step):
        return remote(
            flipped.at[:, z], raw.at[lax.rem(z + RING - step, RING)], f_send.at[step - 1], f_recv.at[step - 1], up
        )

    def columns(j):
        return pl.ds(pl.multiple_of(j * COLS, COLS), COLS)

    def slot(which, first, count):
        return pl.ds(pl.multiple_of(which * band + first, half), count)

    def own_grad(j):
        return pltpu.make_async_copy(g.at[:, columns(j)], gbuf.at[j, slot(z, 0, band)], g_own.at[j])

    def direct(j, side):
        return remote(
            g.at[:, columns(j)], gbuf.at[j, slot(z, 0, band)], d_send.at[j, side], d_recv.at[j, side],
            up if side == 0 else down,
        )

    def direct_in(j, side):
        return remote(
            g.at[:, columns(j)], gbuf.at[j, slot(z_down if side == 0 else z_up, 0, band)],
            d_send.at[j, side], d_recv.at[j, side], up,
        )

    def forward(j, side):
        ref = gbuf.at[j, slot(z_down if side == 0 else z_up, side * half, half)]
        return remote(ref, ref, r_send.at[j, side], r_recv.at[j, side], up if side == 0 else down)

    def forward_in(j, side):
        ref = gbuf.at[j, slot(lax.rem(z + 2, RING), side * half, half)]
        return remote(ref, ref, r_send.at[j, side], r_recv.at[j, side], up)

    def err_in(j):
        return pltpu.make_async_copy(err.at[:, columns(j)], total.at[j], e_in.at[j])

    def error_out(j):
        return pltpu.make_async_copy(total.at[j], error_next.at[:, columns(j)], out_sem.at[j])

    def far(j, side):
        return remote(
            part.at[j, x_far, side], relay.at[j, side], a_send.at[j, side], a_recv.at[j, side],
            right if side == 0 else left,
        )

    def near(j, side):
        return remote(
            part.at[j, x_right if side == 0 else x_left], piece.at[j, side], b_send.at[j, side], b_recv.at[j, side],
            right if side == 0 else left,
        )

    def q_out(step):
        return remote(q_taps, q_near.at[:, x], q_send.at[step - 1], q_recv.at[step - 1], sp_at(x + step, z))

    def q_in(step):
        source = lax.rem(x + RING - step, RING)
        return remote(q_taps, q_near.at[:, source], q_send.at[step - 1], q_recv.at[step - 1], right)

    def t_out(step):
        return remote(
            t_term.at[lax.rem(z + step, RING)], t_near.at[step - 1], t_send.at[step - 1], t_recv.at[step - 1],
            sp_at(x, z + step),
        )

    def p_scatter(d):
        return remote(p_src.at[lax.rem(sp + d, count_sp)], p_near.at[d - 1], s1.at[d - 1], r1.at[d - 1], at_sp(d))

    def p_share(d):
        return remote(p_one, p_far.at[rep], s2.at[d - 1], r2.at[d - 1], at_rep(d))

    def p_share_in(d):
        source = lax.rem(rep + count_rep - d, count_rep)
        return remote(p_one, p_far.at[source], s2.at[d - 1], r2.at[d - 1], at_rep(d))

    def p_gather(d):
        return remote(p_all.at[sp], p_all.at[sp], s3.at[d - 1], r3.at[d - 1], at_sp(d))

    def p_gather_in(d):
        ref = p_all.at[lax.rem(sp + count_sp - d, count_sp)]
        return remote(ref, ref, s3.at[d - 1], r3.at[d - 1], at_sp(d))

    def q_scatter(d):
        return remote(q_src.at[lax.rem(rep + d, count_rep)], q_got.at[d - 1], s4.at[d - 1], r4.at[d - 1], at_rep(d))

    def q_gather(d):
        return remote(q_next.at[rep], q_next.at[rep], s5.at[d - 1], r5.at[d - 1], at_rep(d))

    def q_gather_in(d):
        ref = q_next.at[lax.rem(rep + count_rep - d, count_rep)]
        return remote(ref, ref, s5.at[d - 1], r5.at[d - 1], at_rep(d))

    barrier = pltpu.get_barrier_semaphore()
    for d in range(1, count_sp):
        pl.semaphore_signal(barrier, inc=1, device_id=at_sp(d), device_id_type=MESH)
    for d in range(1, count_rep):
        pl.semaphore_signal(barrier, inc=1, device_id=at_rep(d), device_id_type=MESH)

    own_q = pltpu.make_async_copy(q_taps, q_near.at[:, x], q_copy)
    own_q.start()

    def column_in(i):
        return pltpu.make_async_copy(frames.at[:, columns(i)], local.at[i], l_in.at[i])

    pairs = frames.shape[1] // COLS
    owners = COLS // share
    for i in range(pairs):
        column_in(i).start()
    for i in range(pairs):
        column_in(i).wait()
        turned = local[i].T
        for k in range(owners):
            owner = i * owners + k
            flipped[owner // RING, owner % RING] = turned[k * share : (k + 1) * share]

    pl.semaphore_wait(barrier, count_sp + count_rep - 2)

    for step in (1, 3, 2):
        frames_out(step).start()
        q_out(step).start()
    own_frames = pltpu.make_async_copy(flipped.at[:, z], raw.at[z], f_own)
    own_frames.start()
    for j in range(CHUNKS):
        err_in(j).start()
    for j in range(2):
        direct(j, 0).start()
        direct(j, 1).start()
    for j in range(CHUNKS):
        own_grad(j).start()

    for j in range(CHUNKS):
        err_in(j).wait()
        term = exact_dot(q_own[...], total[j], ((1,), (0,)))
        for h in range(2):
            p_src[2 * j + h] = term[h * (rank // 2) : (h + 1) * (rank // 2)]

    own_q.wait()
    for step in (1, 3, 2):
        q_in(step).wait_recv()
    for tap in range(TAPS):
        q_flip[tap] = q_near[tap].reshape(RING * share, q_near.shape[3]).T

    own_frames.wait()
    for step in (1, 3, 2):
        frames_in(step).wait_recv()

    bottom = raw.at[RING - 1, :, :, band - width : band]
    above = remote(bottom, halo.at[0], h_send.at[0], h_recv.at[0], right)
    below = remote(raw.at[0, :, :, 0:width], halo.at[1], h_send.at[1], h_recv.at[1], left)
    above.start()
    below.start()
    lane = lax.broadcasted_iota(jnp.int32, (RING * share, width), 1)

    def place(row, value):
        at = pl.ds(pl.multiple_of(row * width, width), width)
        wide = value.astype(jnp.float32)
        taps[0, :, at] = jnp.where(lane == 0, 0.0, pltpu.roll(wide, 1, 1)).astype(taps.dtype)
        taps[1, :, at] = value
        taps[2, :, at] = jnp.where(lane == width - 1, 0.0, pltpu.roll(wide, width - 1, 1)).astype(taps.dtype)

    def place_band(which, carry):
        for row in range(band // width):
            value = raw[which, :, :, row * width : (row + 1) * width].reshape(RING * share, width)
            place(which * (band // width) + row + 1, value)
        return carry

    lax.fori_loop(0, RING, place_band, 0)
    rows = RING * band // width
    above.wait()
    below.wait()
    zero = jnp.zeros((RING * share, width), halo.dtype)
    place(0, jnp.where(x == 0, zero, halo[0].reshape(RING * share, width)))
    place(rows + 1, jnp.where(x == RING - 1, zero, halo[1].reshape(RING * share, width)))

    def start_forward(j):
        for side in range(2):
            direct_in(j, side).wait_recv()
            forward(j, side).start()

    start_forward(0)
    for j in range(CHUNKS):
        own_grad(j).wait()

    def t_band(which, carry):
        acc = None
        for a in range(3):
            for b in range(3):
                at = pl.ds(pl.multiple_of(which * band + a * width, width), band)
                term = jnp.dot(q_flip[a * 3 + b], taps[b, :, at], preferred_element_type=jnp.float32)
                acc = term if acc is None else acc + term
        t_term[which] = acc[:rank] + (acc[rank : 2 * rank] + acc[2 * rank : 3 * rank])
        return carry

    lax.fori_loop(0, RING, t_band, 0)
    for step in (1, 3, 2):
        t_out(step).start()

    def p_terms():
        for step in (1, 3, 2):
            t_out(step).wait_recv()
        full = t_term[z] + (t_near[0] + t_near[1] + t_near[2])
        parts = jnp.concatenate(split(full), axis=0)

        def add(j, carry):
            acc = jnp.dot(parts, gbuf[j, slot(z, 0, band)], preferred_element_type=jnp.float32)
            term = acc[:rank] + (acc[rank : 2 * rank] + acc[2 * rank :])
            for h in range(2):
                p_src[2 * j + h] = p_src[2 * j + h] + term[h * (rank // 2) : (h + 1) * (rank // 2)]
            return carry

        lax.fori_loop(0, CHUNKS, add, 0)
        for d in range(1, count_sp):
            p_scatter(d).start()

    def p_sum_sp():
        acc = p_src[sp]
        for d in range(1, count_sp):
            p_scatter(d).wait_recv()
            acc = acc + p_near[d - 1]
        p_one[...] = acc
        p_far[rep] = acc
        for d in range(1, count_rep):
            p_share(d).start()

    def p_sum_rep():
        for d in range(1, count_rep):
            p_share_in(d).wait_recv()
        acc = p_far[0]
        for i in range(1, count_rep):
            acc = acc + p_far[i]
        p_all[sp] = acc
        for d in range(1, count_sp):
            p_gather(d).start()

    def p_chunk(j):
        return jnp.concatenate([p_all[2 * j], p_all[2 * j + 1]], axis=0)

    def orthogonal():
        for d in range(1, count_sp):
            p_gather_in(d).wait_recv()
        gram = jnp.zeros((rank, rank), jnp.float32)
        for j in range(CHUNKS):
            block = p_chunk(j)
            gram = gram + exact_dot(block, block, ((1,), (1,)))
        row_at = lax.broadcasted_iota(jnp.int32, (rank, rank), 0)
        col_at = lax.broadcasted_iota(jnp.int32, (rank, rank), 1)
        work[:, :rank] = gram
        work[:, rank : 2 * rank] = jnp.where(row_at == col_at, 1.0, 0.0)
        shape = (rank, 2 * rank)
        line = lax.broadcasted_iota(jnp.int32, shape, 0)
        spot = lax.broadcasted_iota(jnp.int32, shape, 1)

        def eliminate(k, carry):
            state = work[:, : 2 * rank]
            column = jnp.sum(jnp.where(spot == k, state, 0.0), axis=1, keepdims=True)
            pivot = jnp.sum(jnp.where(line == k, state, 0.0), axis=0, keepdims=True)
            diagonal = jnp.sum(jnp.where((spot == k) & (line == k), state, 0.0), axis=(0, 1), keepdims=True)
            inverse = 1.0 / jnp.sqrt(diagonal)
            pivot = pivot * inverse
            work[:, : 2 * rank] = jnp.where(
                line > k, state - (column * inverse) * pivot, jnp.where(line == k, pivot, state)
            )
            return carry

        lax.fori_loop(0, rank, eliminate, 0)
        lower_inverse = jnp.where(col_at <= row_at, work[:, rank : 2 * rank], 0.0)
        for j in range(CHUNKS):
            p_ortho[j] = exact_dot(lower_inverse, p_chunk(j), ((1,), (0,)))
        q_sum[...] = jnp.zeros_like(q_sum)

    def add_q(k):
        q_sum[...] = q_sum[...] + exact_dot(p_ortho[k], total[k], ((1,), (1,)))

    def step(j, carry):
        @pl.when(j + 2 < CHUNKS)
        def _():
            direct(j + 2, 0).start()
            direct(j + 2, 1).start()

        @pl.when(j + 1 < CHUNKS)
        def _():
            start_forward(j + 1)

        @pl.when(j < CHUNKS)
        def _():
            forward_in(j, 0).wait_recv()
            forward_in(j, 1).wait_recv()
            depth = gbuf.shape[1]
            for a in range(3):
                for b in range(3):
                    product = jnp.dot(
                        taps[b, :, a * width : a * width + depth], gbuf[j], preferred_element_type=jnp.float32
                    )
                    count = part.shape[4]
                    for owner in range(RING):
                        for side in range(2):
                            first = (owner * 2 + side) * count
                            part[j, owner, side, a * 3 + b] = product[first : first + count]
            far(j, 0).start()
            far(j, 1).start()

        @pl.when((j >= 1) & (j <= CHUNKS))
        def _():
            k = j - 1
            far(k, 0).wait_recv()
            part[k, x_right, 0] = part[k, x_right, 0] + relay[k, 0]
            near(k, 0).start()
            far(k, 1).wait_recv()
            part[k, x_left, 1] = part[k, x_left, 1] + relay[k, 1]
            near(k, 1).start()

        pl.when(j == P_AT)(p_terms)
        pl.when(j == P_AT + 1)(p_sum_sp)
        pl.when(j == P_AT + 2)(p_sum_rep)
        pl.when(j == P_AT + 3)(orthogonal)

        @pl.when(j >= 2)
        def _():
            k = j - 2
            near(k, 0).wait_recv()
            near(k, 1).wait_recv()
            count = part.shape[4]
            for side in range(2):
                for tap in range(TAPS):
                    at = pl.ds(side * count * TAPS + tap, count, stride=TAPS)
                    total[k, at, :] = (
                        total[k, at, :] + part[k, x, side, tap] + (piece[k, 0, side, tap] + piece[k, 1, side, tap])
                    )

            @pl.when(j >= P_AT + 3)
            def _():
                add_q(k)

        @pl.when(j == P_AT + 3)
        def _():
            for k in range(P_AT + 1):
                add_q(k)

        return carry

    lax.fori_loop(0, CHUNKS + 2, step, 0)

    lines = rank // count_rep
    for i in range(count_rep):
        q_src[i] = q_sum[i * lines : (i + 1) * lines]
    for d in range(1, count_rep):
        q_scatter(d).start()
    acc = q_src[rep]
    for d in range(1, count_rep):
        q_scatter(d).wait_recv()
        acc = acc + q_got[d - 1]
    q_next[rep] = acc * (1.0 / count_rep)
    for d in range(1, count_rep):
        q_gather(d).start()
    for d in range(1, count_rep):
        q_gather_in(d).wait_recv()
    for i in range(count_rep):
        q_flat[i * lines : (i + 1) * lines] = q_next[i]

    q0, q1, q2 = split(q_flat[...])
    q_side = jnp.concatenate([q0, q0, q0, q1, q1, q2], axis=0).T

    def finish(j, carry):
        p0, p1, p2 = split(p_ortho[j])
        p_side = jnp.concatenate([p0, p1, p2, p0, p1, p0], axis=0)
        total[j] = total[j] - jnp.dot(q_side, p_side, preferred_element_type=jnp.float32)
        error_out(j).start()
        for side in range(2):
            direct(j, side).wait_send()
            forward(j, side).wait_send()
            far(j, side).wait_send()
            near(j, side).wait_send()
        return carry

    lax.fori_loop(0, CHUNKS, finish, 0)
    for step_ in (1, 3, 2):
        frames_out(step_).wait_send()
        q_out(step_).wait_send()
        t_out(step_).wait_send()
    for d in range(1, count_sp):
        p_scatter(d).wait_send()
        p_gather(d).wait_send()
    for d in range(1, count_rep):
        p_share(d).wait_send()
        q_scatter(d).wait_send()
        q_gather(d).wait_send()
    for j in range(CHUNKS):
        error_out(j).wait()


def compressed_step(count_rep, frames, g, err, q_own, q_taps):
    band, chans = g.shape
    width = band // 4
    rows = err.shape[0]
    rank = q_own.shape[0]
    count_sp = RING * RING
    share = chans // count_sp
    per_side = share // 2
    dma = pltpu.SemaphoreType.DMA
    two = dma((CHUNKS, 2))
    f32, bf16 = jnp.float32, jnp.bfloat16
    any_spec, vmem_spec = pl.BlockSpec(memory_space=pl.ANY), pl.BlockSpec(memory_space=pltpu.VMEM)
    p_block = (rank // 2, COLS)
    q_block = (rank // count_rep, rows)
    return pl.pallas_call(
        functools.partial(step_kernel, count_rep),
        out_shape=(
            jax.ShapeDtypeStruct((rows, chans), f32),
            jax.ShapeDtypeStruct((count_rep, *q_block), f32),
        ),
        in_specs=[any_spec, any_spec, any_spec, vmem_spec, vmem_spec],
        out_specs=(any_spec, vmem_spec),
        scratch_shapes=[
            pltpu.VMEM((chans // COLS, band, COLS), bf16),
            pltpu.VMEM((RING, RING, share, band), bf16),
            pltpu.VMEM((RING, RING, share, band), bf16),
            pltpu.VMEM((2, RING, share, width), bf16),
            pltpu.VMEM((3, RING * share, RING * band + 2 * width), bf16),
            pltpu.VMEM((CHUNKS, RING * band, COLS), bf16),
            pltpu.VMEM((CHUNKS, RING, 2, TAPS, per_side, COLS), f32),
            pltpu.VMEM((CHUNKS, 2, TAPS, per_side, COLS), f32),
            pltpu.VMEM((CHUNKS, 2, 2, TAPS, per_side, COLS), f32),
            pltpu.VMEM((CHUNKS, rows, COLS), f32),
            pltpu.VMEM((TAPS, RING, share, q_taps.shape[2]), bf16),
            pltpu.VMEM((TAPS, q_taps.shape[2], RING * share), bf16),
            pltpu.VMEM((RING, rank, band), f32),
            pltpu.VMEM((RING - 1, rank, band), f32),
            pltpu.VMEM((count_sp, *p_block), f32),
            pltpu.VMEM((count_sp - 1, *p_block), f32),
            pltpu.VMEM(p_block, f32),
            pltpu.VMEM((count_rep, *p_block), f32),
            pltpu.VMEM((count_sp, *p_block), f32),
            pltpu.VMEM((CHUNKS, rank, COLS), f32),
            pltpu.VMEM((rank, 128), f32),
            pltpu.VMEM((count_rep, *q_block), f32),
            pltpu.VMEM((count_rep - 1, *q_block), f32),
            pltpu.VMEM((rank, rows), f32),
            pltpu.VMEM((rank, rows), f32),
            dma((chans // COLS,)), dma((3,)), dma((3,)), dma, dma((2,)), dma((2,)), dma((CHUNKS,)), dma((CHUNKS,)),
            two, two, two, two, two, two, two, two, dma((CHUNKS,)),
            dma((3,)), dma((3,)), dma, dma((3,)), dma((3,)),
            dma((count_sp - 1,)), dma((count_sp - 1,)), dma((count_rep - 1,)), dma((count_rep - 1,)),
            dma((count_sp - 1,)), dma((count_sp - 1,)), dma((count_rep - 1,)), dma((count_rep - 1,)),
            dma((count_rep - 1,)), dma((count_rep - 1,)),
        ],
        compiler_params=pltpu.CompilerParams(
            collective_id=0, has_side_effects=True, vmem_limit_bytes=58 * 1024 * 1024
        ),
        cost_estimate=pl.CostEstimate(flops=2 * rows * 16 * chans * band, bytes_accessed=10**7, transcendentals=0),
        name="compressed_step",
    )(frames, g, err, q_own, q_taps)


def per_device(count_rep, frames, out_grad, error_prev, q_prev):
    band_rows, width, chans = frames.shape[1:]
    band = band_rows * width
    rank, rows = q_prev.shape
    by_tap = q_prev.reshape(rank, rows // TAPS, TAPS).transpose(2, 1, 0)
    high = lax.reduce_precision(by_tap, 8, 7)
    middle = lax.reduce_precision(by_tap - high, 8, 7)
    low = by_tap - high - middle
    parts = jnp.concatenate([high, middle, low, jnp.zeros_like(low)], axis=2)[:, :, :128]
    error_next, q_next = compressed_step(
        count_rep,
        frames[0].reshape(band, chans),
        out_grad[0].reshape(band, chans),
        error_prev[0],
        q_prev,
        parts.astype(jnp.bfloat16),
    )
    return (error_next[None], q_next.reshape(rank, rows))


def solution(mesh):
    placed = (
        P("rep", "sp", None, None),
        P("rep", "sp", None, None),
        P("rep", "sp", None),
        P(None, "sp"),
    )
    return jax.shard_map(
        functools.partial(per_device, mesh.shape["rep"]),
        mesh=mesh,
        in_specs=placed,
        out_specs=(P("rep", "sp", None), P(None, "sp")),
        check_vma=False,
    )
```

time: 573 us -> 170 us (0.30)
  waiting for transfers between devices: 431 us -> 0 us
  Pallas kernels: 0 us -> 162 us
  local copies, waits for them, and re-layouts: 63.6 us -> 6.05 us
  matrix products: 46.2 us -> 0 us
  between operations: 13.8 us -> 0.67 us
  other arithmetic: 11.1 us -> 0.95 us
  starting transfers between devices: 6.21 us -> 0 us
    reduce_scatter x1 -> x0, waiting for transfers between devices: 220 us -> none  [per_device(): lax.psum_scatter(lax.dot_general(cols, flat_grad, (((0,), (0,)), ((), ())...]
    psum x3 -> x0, waiting for transfers between devices: 198 us -> none  [the longest x2 141 us: per_device(): p_total = lax.psum(lax.psum(p_term, 'sp'), 'rep')]
    pallas_call x0 -> x1, Pallas kernels: none -> 162 us  [compressed_step(): pl.pallas_call(functools.partial(step_kernel, count_rep), out_shape=(jax....]
    dot_general x5 -> x0, matrix products: 45 us -> none  [the longest x1 28.1 us: per_device(): lax.dot_general(cols, flat_grad, (((0,), (0,)), ((), ())), preferred_elem...]
    another operation x2 -> x0, local copies, waits for them, and re-layouts: 31.1 us -> none  [make_patches(): stacked = jnp.stack(taps, axis=-1)]
    unnamed x17 -> x2, local copies, waits for them, and re-layouts: 31 us -> 4.39 us
    ppermute x2 -> x0, waiting for transfers between devices: 13.4 us -> none  [the longest x1 9.24 us: with_halo(): lax.ppermute(lax.slice_in_dim(block, block.shape[dim] - width, None, axis...]
    another operation x5 -> x1, other arithmetic: 6.68 us -> 0.14 us  [the longest x3 3.6 us: per_device(): lower = jnp.linalg.cholesky(gram)]
  transfers between devices with their start and end apart: 6 -> 0, of which waited for: 6 -> 0; matrix products, arithmetic and copies ran while one was open for 0% -> 0% of each run, Pallas kernels for 0% -> 0%
where the time goes in v1:
time: 170 us; the launch traced here: 169 us
  Pallas kernels  162 us (95%)
  local copies, waits for them, and re-layouts  6.05 us (4%)
    pallas_call x1, Pallas kernels, compressed_step(): pl.pallas_call(functools.partial(step_kernel, count_rep), out_shape=(jax....  162 us
    unnamed x2, local copies, waits for them, and re-layouts  4.39 us

profile of v1, /device:TPU:1, one launch (start us, length us, event | category | flops | bytes accessed | tf_op | source)
XLA Modules:
  0.0 169.2 jit_solution(6191321098852777494)
XLA Ops:
  0.6 0.1 pad.3.clone
  0.7 1.0 copy.8
  1.8 0.1 reduce-precision_convert_fusion.1
  1.9 0.8 maximum_maximum_fusion.q_taps
  2.8 161.6 %compressed_step.1 = (f32[576,1024]{1,0:T(8,128)}, f32[8,4,576]{2,1,0:T(4,128)}) custom-call(bf16[1024,1024]{1,0:T(8,128)(2,1)} %bitcast.15, bf16[1024,1024]{1,0:T(8,128)(2,1)} %bitcast.16, f32[576,1024]{1,0:T(8,128)} %bitcast.14, f32[32,576]{1,0:T(8,128)} %q_own.1, bf16[9,64,128]{2,1,0:T(8,128)(2,1)} %maximum_maximum_fusion.q_taps), custom_call_target="tpu_custom_call" | custom-call | flops 19327352832 | bytes 10000000 | tf_op jit(solution)/shard_map/compressed_step/pallas_call | solution.py:479
  164.3 1.6 reshape.11
  165.9 3.4 %copy.14 = f32[1,576,1024]{2,1,0:T(8,128)} copy(f32[1,576,1024]{2,1,0:T(8,128)} %bitcast.13) | data formatting | bytes 4718592
  (2 shorter events, 0.0 us)

commit v2 on v1

--- a/solution.py
+++ b/solution.py
@@ -12,7 +12,7 @@
 CHUNKS = 8
 COLS = 128
 TAPS = 9
-P_AT = 1
+P_AT = 2
 
 
 def sp_at(x, z):
@@ -40,9 +40,9 @@
 
 
 def step_kernel(
-    count_rep, frames, g, err, q_own, q_taps, error_next, q_next,
-    local, flipped, raw, halo, taps, gbuf, part, relay, piece, total,
-    q_near, q_flip, t_term, t_near, p_src, p_near, p_one, p_far, p_all, p_ortho, work, q_src, q_got, q_sum, q_flat,
+    count_rep, frames, g, err, q_own, memory, q_next, p_ortho,
+    local, q_turned, q_taps, flipped, raw, halo, taps, gbuf, part, relay, piece, total,
+    q_near, q_flip, t_term, t_near, p_src, p_near, p_one, p_far, p_all, work, q_src, q_got, q_sum,
     l_in, f_send, f_recv, f_own, h_send, h_recv, e_in, g_own,
     d_send, d_recv, r_send, r_recv, a_send, a_recv, b_send, b_recv, out_sem,
     q_send, q_recv, q_copy, t_send, t_recv, s1, r1, s2, r2, s3, r3, s4, r4, s5, r5,
@@ -109,19 +109,21 @@
     def err_in(j):
         return pltpu.make_async_copy(err.at[:, columns(j)], total.at[j], e_in.at[j])
 
-    def error_out(j):
-        return pltpu.make_async_copy(total.at[j], error_next.at[:, columns(j)], out_sem.at[j])
-
-    def far(j, side):
+    def mem_out(j):
+        return pltpu.make_async_copy(total.at[j], memory.at[:, columns(j)], out_sem.at[j])
+
+    def far(j, side, group):
+        some = pl.ds(group * 3, 3)
         return remote(
-            part.at[j, x_far, side], relay.at[j, side], a_send.at[j, side], a_recv.at[j, side],
-            right if side == 0 else left,
+            part.at[j, x_far, side, some], relay.at[j, side, some], a_send.at[j, side, group],
+            a_recv.at[j, side, group], right if side == 0 else left,
         )
 
-    def near(j, side):
+    def near(j, side, group):
+        some = pl.ds(group * 3, 3)
         return remote(
-            part.at[j, x_right if side == 0 else x_left], piece.at[j, side], b_send.at[j, side], b_recv.at[j, side],
-            right if side == 0 else left,
+            part.at[j, x_right if side == 0 else x_left, :, some], piece.at[j, side, :, some],
+            b_send.at[j, side, group], b_recv.at[j, side, group], right if side == 0 else left,
         )
 
     def q_out(step):
@@ -170,9 +172,6 @@
     for d in range(1, count_rep):
         pl.semaphore_signal(barrier, inc=1, device_id=at_rep(d), device_id_type=MESH)
 
-    own_q = pltpu.make_async_copy(q_taps, q_near.at[:, x], q_copy)
-    own_q.start()
-
     def column_in(i):
         return pltpu.make_async_copy(frames.at[:, columns(i)], local.at[i], l_in.at[i])
 
@@ -180,49 +179,35 @@
     owners = COLS // share
     for i in range(pairs):
         column_in(i).start()
+    pl.semaphore_wait(barrier, count_sp + count_rep - 2)
+    direct(0, 0).start()
+    direct(0, 1).start()
+
     for i in range(pairs):
         column_in(i).wait()
         turned = local[i].T
         for k in range(owners):
             owner = i * owners + k
             flipped[owner // RING, owner % RING] = turned[k * share : (k + 1) * share]
-
-    pl.semaphore_wait(barrier, count_sp + count_rep - 2)
-
     for step in (1, 3, 2):
         frames_out(step).start()
-        q_out(step).start()
     own_frames = pltpu.make_async_copy(flipped.at[:, z], raw.at[z], f_own)
     own_frames.start()
     for j in range(CHUNKS):
         err_in(j).start()
-    for j in range(2):
-        direct(j, 0).start()
-        direct(j, 1).start()
-    for j in range(CHUNKS):
         own_grad(j).start()
 
-    for j in range(CHUNKS):
-        err_in(j).wait()
-        term = exact_dot(q_own[...], total[j], ((1,), (0,)))
-        for h in range(2):
-            p_src[2 * j + h] = term[h * (rank // 2) : (h + 1) * (rank // 2)]
-
-    own_q.wait()
+    thirds = [third.astype(jnp.float32) for third in split(q_own[...])]
+    lanes = q_taps.shape[2]
+    thirds.append(jnp.zeros((lanes - 3 * rank, q_own.shape[1]), jnp.float32))
+    q_turned[...] = jnp.concatenate(thirds, axis=0).T
+    for tap in range(TAPS):
+        q_taps[tap] = q_turned[pl.ds(tap, share, stride=TAPS), :].astype(jnp.bfloat16)
     for step in (1, 3, 2):
-        q_in(step).wait_recv()
-    for tap in range(TAPS):
-        q_flip[tap] = q_near[tap].reshape(RING * share, q_near.shape[3]).T
-
-    own_frames.wait()
-    for step in (1, 3, 2):
-        frames_in(step).wait_recv()
-
-    bottom = raw.at[RING - 1, :, :, band - width : band]
-    above = remote(bottom, halo.at[0], h_send.at[0], h_recv.at[0], right)
-    below = remote(raw.at[0, :, :, 0:width], halo.at[1], h_send.at[1], h_recv.at[1], left)
-    above.start()
-    below.start()
+        q_out(step).start()
+    own_q = pltpu.make_async_copy(q_taps, q_near.at[:, x], q_copy)
+    own_q.start()
+
     lane = lax.broadcasted_iota(jnp.int32, (RING * share, width), 1)
 
     def place(row, value):
@@ -232,13 +217,47 @@
         taps[1, :, at] = value
         taps[2, :, at] = jnp.where(lane == width - 1, 0.0, pltpu.roll(wide, width - 1, 1)).astype(taps.dtype)
 
-    def place_band(which, carry):
-        for row in range(band // width):
-            value = raw[which, :, :, row * width : (row + 1) * width].reshape(RING * share, width)
-            place(which * (band // width) + row + 1, value)
-        return carry
-
-    lax.fori_loop(0, RING, place_band, 0)
+    def place_band(which):
+        def place_row(row, carry):
+            at = pl.ds(pl.multiple_of(row * width, width), width)
+            place(which * (band // width) + row + 1, raw[which, :, :, at].reshape(RING * share, width))
+            return carry
+
+        lax.fori_loop(0, band // width, place_row, 0)
+
+    def start_forward(j):
+        for side in range(2):
+            direct_in(j, side).wait_recv()
+            forward(j, side).start()
+
+    def start_direct(j):
+        for side in range(2):
+            direct(j, side).start()
+
+    start_forward(0)
+    own_frames.wait()
+    place_band(z)
+
+    for j in range(CHUNKS):
+        err_in(j).wait()
+        term = exact_dot(q_own[...], total[j], ((1,), (0,)))
+        for h in range(2):
+            p_src[2 * j + h] = term[h * (rank // 2) : (h + 1) * (rank // 2)]
+
+    frames_in(1).wait_recv()
+    frames_in(3).wait_recv()
+    start_direct(1)
+    place_band(z_down)
+    place_band(z_up)
+    frames_in(2).wait_recv()
+    start_direct(2)
+
+    bottom = raw.at[RING - 1, :, :, band - width : band]
+    above = remote(bottom, halo.at[0], h_send.at[0], h_recv.at[0], right)
+    below = remote(raw.at[0, :, :, 0:width], halo.at[1], h_send.at[1], h_recv.at[1], left)
+    above.start()
+    below.start()
+    place_band(lax.rem(z + 2, RING))
     rows = RING * band // width
     above.wait()
     below.wait()
@@ -246,16 +265,11 @@
     place(0, jnp.where(x == 0, zero, halo[0].reshape(RING * share, width)))
     place(rows + 1, jnp.where(x == RING - 1, zero, halo[1].reshape(RING * share, width)))
 
-    def start_forward(j):
-        for side in range(2):
-            direct_in(j, side).wait_recv()
-            forward(j, side).start()
-
-    start_forward(0)
+    start_forward(1)
     for j in range(CHUNKS):
         own_grad(j).wait()
 
-    def t_band(which, carry):
+    def t_band(which):
         acc = None
         for a in range(3):
             for b in range(3):
@@ -263,11 +277,24 @@
                 term = jnp.dot(q_flip[a * 3 + b], taps[b, :, at], preferred_element_type=jnp.float32)
                 acc = term if acc is None else acc + term
         t_term[which] = acc[:rank] + (acc[rank : 2 * rank] + acc[2 * rank : 3 * rank])
-        return carry
-
-    lax.fori_loop(0, RING, t_band, 0)
-    for step in (1, 3, 2):
-        t_out(step).start()
+
+    def t_start():
+        own_q.wait()
+        for step in (1, 3, 2):
+            q_in(step).wait_recv()
+        for tap in range(TAPS):
+            q_flip[tap] = q_near[tap].reshape(RING * share, lanes).T
+
+    def t_bands(first):
+        def one(i, carry):
+            t_band(first + i)
+            return carry
+
+        lax.fori_loop(0, RING // 2, one, 0)
+
+    def t_finish():
+        for step in (1, 3, 2):
+            t_out(step).start()
 
     def p_terms():
         for step in (1, 3, 2):
@@ -326,9 +353,9 @@
 
         def eliminate(k, carry):
             state = work[:, : 2 * rank]
+            pivot = work[pl.ds(k, 1), : 2 * rank]
             column = jnp.sum(jnp.where(spot == k, state, 0.0), axis=1, keepdims=True)
-            pivot = jnp.sum(jnp.where(line == k, state, 0.0), axis=0, keepdims=True)
-            diagonal = jnp.sum(jnp.where((spot == k) & (line == k), state, 0.0), axis=(0, 1), keepdims=True)
+            diagonal = jnp.sum(jnp.where(spot[:1] == k, pivot, 0.0), axis=1, keepdims=True)
             inverse = 1.0 / jnp.sqrt(diagonal)
             pivot = pivot * inverse
             work[:, : 2 * rank] = jnp.where(
@@ -346,14 +373,13 @@
         q_sum[...] = q_sum[...] + exact_dot(p_ortho[k], total[k], ((1,), (1,)))
 
     def step(j, carry):
+        @pl.when(j + 3 < CHUNKS)
+        def _():
+            start_direct(j + 3)
+
         @pl.when(j + 2 < CHUNKS)
         def _():
-            direct(j + 2, 0).start()
-            direct(j + 2, 1).start()
-
-        @pl.when(j + 1 < CHUNKS)
-        def _():
-            start_forward(j + 1)
+            start_forward(j + 2)
 
         @pl.when(j < CHUNKS)
         def _():
@@ -370,18 +396,30 @@
                         for side in range(2):
                             first = (owner * 2 + side) * count
                             part[j, owner, side, a * 3 + b] = product[first : first + count]
-            far(j, 0).start()
-            far(j, 1).start()
+                far(j, 0, a).start()
+                far(j, 1, a).start()
 
         @pl.when((j >= 1) & (j <= CHUNKS))
         def _():
             k = j - 1
-            far(k, 0).wait_recv()
-            part[k, x_right, 0] = part[k, x_right, 0] + relay[k, 0]
-            near(k, 0).start()
-            far(k, 1).wait_recv()
-            part[k, x_left, 1] = part[k, x_left, 1] + relay[k, 1]
-            near(k, 1).start()
+            for group in range(3):
+                some = pl.ds(group * 3, 3)
+                far(k, 0, group).wait_recv()
+                part[k, x_right, 0, some] = part[k, x_right, 0, some] + relay[k, 0, some]
+                near(k, 0, group).start()
+                far(k, 1, group).wait_recv()
+                part[k, x_left, 1, some] = part[k, x_left, 1, some] + relay[k, 1, some]
+                near(k, 1, group).start()
+
+        @pl.when(j == 0)
+        def _():
+            t_start()
+            t_bands(0)
+
+        @pl.when(j == 1)
+        def _():
+            t_bands(RING // 2)
+            t_finish()
 
         pl.when(j == P_AT)(p_terms)
         pl.when(j == P_AT + 1)(p_sum_sp)
@@ -391,8 +429,9 @@
         @pl.when(j >= 2)
         def _():
             k = j - 2
-            near(k, 0).wait_recv()
-            near(k, 1).wait_recv()
+            for group in range(3):
+                near(k, 0, group).wait_recv()
+                near(k, 1, group).wait_recv()
             count = part.shape[4]
             for side in range(2):
                 for tap in range(TAPS):
@@ -400,6 +439,8 @@
                     total[k, at, :] = (
                         total[k, at, :] + part[k, x, side, tap] + (piece[k, 0, side, tap] + piece[k, 1, side, tap])
                     )
+
+            mem_out(k).start()
 
             @pl.when(j >= P_AT + 3)
             def _():
@@ -428,22 +469,15 @@
         q_gather(d).start()
     for d in range(1, count_rep):
         q_gather_in(d).wait_recv()
-    for i in range(count_rep):
-        q_flat[i * lines : (i + 1) * lines] = q_next[i]
-
-    q0, q1, q2 = split(q_flat[...])
-    q_side = jnp.concatenate([q0, q0, q0, q1, q1, q2], axis=0).T
 
     def finish(j, carry):
-        p0, p1, p2 = split(p_ortho[j])
-        p_side = jnp.concatenate([p0, p1, p2, p0, p1, p0], axis=0)
-        total[j] = total[j] - jnp.dot(q_side, p_side, preferred_element_type=jnp.float32)
-        error_out(j).start()
         for side in range(2):
             direct(j, side).wait_send()
             forward(j, side).wait_send()
-            far(j, side).wait_send()
-            near(j, side).wait_send()
+            for group in range(3):
+                far(j, side, group).wait_send()
+                near(j, side, group).wait_send()
+        mem_out(j).wait()
         return carry
 
     lax.fori_loop(0, CHUNKS, finish, 0)
@@ -458,11 +492,9 @@
         p_share(d).wait_send()
         q_scatter(d).wait_send()
         q_gather(d).wait_send()
-    for j in range(CHUNKS):
-        error_out(j).wait()
-
-
-def compressed_step(count_rep, frames, g, err, q_own, q_taps):
+
+
+def compressed_step(count_rep, frames, g, err, q_own):
     band, chans = g.shape
     width = band // 4
     rows = err.shape[0]
@@ -471,7 +503,7 @@
     share = chans // count_sp
     per_side = share // 2
     dma = pltpu.SemaphoreType.DMA
-    two = dma((CHUNKS, 2))
+    two, three = dma((CHUNKS, 2)), dma((CHUNKS, 2, 3))
     f32, bf16 = jnp.float32, jnp.bfloat16
     any_spec, vmem_spec = pl.BlockSpec(memory_space=pl.ANY), pl.BlockSpec(memory_space=pltpu.VMEM)
     p_block = (rank // 2, COLS)
@@ -481,11 +513,14 @@
         out_shape=(
             jax.ShapeDtypeStruct((rows, chans), f32),
             jax.ShapeDtypeStruct((count_rep, *q_block), f32),
+            jax.ShapeDtypeStruct((CHUNKS, rank, COLS), f32),
         ),
-        in_specs=[any_spec, any_spec, any_spec, vmem_spec, vmem_spec],
-        out_specs=(any_spec, vmem_spec),
+        in_specs=[any_spec, any_spec, any_spec, vmem_spec],
+        out_specs=(any_spec, vmem_spec, vmem_spec),
         scratch_shapes=[
             pltpu.VMEM((chans // COLS, band, COLS), bf16),
+            pltpu.VMEM((rows, 128), f32),
+            pltpu.VMEM((TAPS, share, 128), bf16),
             pltpu.VMEM((RING, RING, share, band), bf16),
             pltpu.VMEM((RING, RING, share, band), bf16),
             pltpu.VMEM((2, RING, share, width), bf16),
@@ -495,8 +530,8 @@
             pltpu.VMEM((CHUNKS, 2, TAPS, per_side, COLS), f32),
             pltpu.VMEM((CHUNKS, 2, 2, TAPS, per_side, COLS), f32),
             pltpu.VMEM((CHUNKS, rows, COLS), f32),
-            pltpu.VMEM((TAPS, RING, share, q_taps.shape[2]), bf16),
-            pltpu.VMEM((TAPS, q_taps.shape[2], RING * share), bf16),
+            pltpu.VMEM((TAPS, RING, share, 128), bf16),
+            pltpu.VMEM((TAPS, 128, RING * share), bf16),
             pltpu.VMEM((RING, rank, band), f32),
             pltpu.VMEM((RING - 1, rank, band), f32),
             pltpu.VMEM((count_sp, *p_block), f32),
@@ -504,14 +539,12 @@
             pltpu.VMEM(p_block, f32),
             pltpu.VMEM((count_rep, *p_block), f32),
             pltpu.VMEM((count_sp, *p_block), f32),
-            pltpu.VMEM((CHUNKS, rank, COLS), f32),
             pltpu.VMEM((rank, 128), f32),
             pltpu.VMEM((count_rep, *q_block), f32),
             pltpu.VMEM((count_rep - 1, *q_block), f32),
             pltpu.VMEM((rank, rows), f32),
-            pltpu.VMEM((rank, rows), f32),
             dma((chans // COLS,)), dma((3,)), dma((3,)), dma, dma((2,)), dma((2,)), dma((CHUNKS,)), dma((CHUNKS,)),
-            two, two, two, two, two, two, two, two, dma((CHUNKS,)),
+            two, two, two, two, three, three, three, three, dma((CHUNKS,)),
             dma((3,)), dma((3,)), dma, dma((3,)), dma((3,)),
             dma((count_sp - 1,)), dma((count_sp - 1,)), dma((count_rep - 1,)), dma((count_rep - 1,)),
             dma((count_sp - 1,)), dma((count_sp - 1,)), dma((count_rep - 1,)), dma((count_rep - 1,)),
@@ -522,27 +555,60 @@
         ),
         cost_estimate=pl.CostEstimate(flops=2 * rows * 16 * chans * band, bytes_accessed=10**7, transcendentals=0),
         name="compressed_step",
-    )(frames, g, err, q_own, q_taps)
+    )(frames, g, err, q_own)
+
+
+def feedback_kernel(memory, q_parts, p_ortho, error_next, q_next, q_side):
+    count, lines, rows = q_parts.shape
+
+    @pl.when(pl.program_id(0) == 0)
+    def _():
+        for i in range(count):
+            q_next[i * lines : (i + 1) * lines] = q_parts[i]
+        q0, q1, q2 = split(q_next[...])
+        q_side[...] = jnp.concatenate([q0, q0, q0, q1, q1, q2], axis=0).T
+
+    for i in range(p_ortho.shape[0]):
+        p0, p1, p2 = split(p_ortho[i])
+        p_side = jnp.concatenate([p0, p1, p2, p0, p1, p0], axis=0)
+        at = slice(i * COLS, (i + 1) * COLS)
+        error_next[:, at] = memory[:, at] - jnp.dot(q_side[...], p_side, preferred_element_type=jnp.float32)
+
+
+def feedback(memory, q_parts, p_ortho):
+    rows, chans = memory.shape
+    count, lines, _ = q_parts.shape
+    rank = count * lines
+    per_block = 2
+    block = (rows, per_block * COLS)
+    return pl.pallas_call(
+        feedback_kernel,
+        grid=(chans // block[1],),
+        out_shape=(jax.ShapeDtypeStruct(memory.shape, jnp.float32), jax.ShapeDtypeStruct((rank, rows), jnp.float32)),
+        in_specs=[
+            pl.BlockSpec(block, lambda i: (0, i)),
+            pl.BlockSpec(q_parts.shape, lambda i: (0, 0, 0)),
+            pl.BlockSpec((per_block, rank, COLS), lambda i: (i, 0, 0)),
+        ],
+        out_specs=(pl.BlockSpec(block, lambda i: (0, i)), pl.BlockSpec((rank, rows), lambda i: (0, 0))),
+        scratch_shapes=[pltpu.VMEM((rows, 6 * rank), jnp.bfloat16)],
+        compiler_params=pltpu.CompilerParams(vmem_limit_bytes=32 * 1024 * 1024),
+        name="feedback",
+    )(memory, q_parts, p_ortho)
 
 
 def per_device(count_rep, frames, out_grad, error_prev, q_prev):
     band_rows, width, chans = frames.shape[1:]
     band = band_rows * width
-    rank, rows = q_prev.shape
-    by_tap = q_prev.reshape(rank, rows // TAPS, TAPS).transpose(2, 1, 0)
-    high = lax.reduce_precision(by_tap, 8, 7)
-    middle = lax.reduce_precision(by_tap - high, 8, 7)
-    low = by_tap - high - middle
-    parts = jnp.concatenate([high, middle, low, jnp.zeros_like(low)], axis=2)[:, :, :128]
-    error_next, q_next = compressed_step(
+    memory, q_parts, p_ortho = compressed_step(
         count_rep,
         frames[0].reshape(band, chans),
         out_grad[0].reshape(band, chans),
         error_prev[0],
         q_prev,
-        parts.astype(jnp.bfloat16),
     )
-    return (error_next[None], q_next.reshape(rank, rows))
+    error_next, q_next = feedback(memory, q_parts, p_ortho)
+    return (error_next[None], q_next)
 
 
 def solution(mesh):

time: 170 us -> 166 us (0.976)
  local copies, waits for them, and re-layouts: 6.05 us -> 3.45 us
    pallas_call x0 -> x1, Pallas kernels: none -> 2.87 us  [feedback(): pl.pallas_call(feedback_kernel, grid=(chans // block[1],), out_shape=(jax...]
    pallas_call x1, Pallas kernels: 162 us -> 159 us  [compressed_step(): pl.pallas_call(functools.partial(step_kernel, count_rep), out_shape=(jax....]
    unnamed x2 -> x6, local copies, waits for them, and re-layouts: 4.39 us -> 3.45 us
where the time goes in v2:
time: 166 us
  Pallas kernels  162 us (98%)
  local copies, waits for them, and re-layouts  3.45 us (2%)
    pallas_call x1, Pallas kernels, compressed_step(): pl.pallas_call(functools.partial(step_kernel, count_rep), out_shape=(jax....  159 us
    unnamed x6, local copies, waits for them, and re-layouts  3.45 us

profile of v2, /device:TPU:1, one launch (start us, length us, event | category | flops | bytes accessed | tf_op | source)
XLA Modules:
  0.0 165.9 jit_solution(8880188377430660672)
XLA Ops:
  0.6 158.9 %compressed_step.1 = (f32[576,1024]{1,0:T(8,128)}, f32[8,4,576]{2,1,0:T(4,128)}, f32[8,32,128]{2,1,0:T(8,128)}) custom-call(bf16[1024,1024]{1,0:T(8,128)(2,1)} %bitcast.6, bf16[1024,1024]{1,0:T(8,128)(2,1)} %bitcast.7, f32[576,1024]{1,0:T(8,128)} %bitcast.4, f32[32,576]{1,0:T(8,128)} %q_own.1), custom_call_target="tpu_custom_call" | custom-call | flops 19327352832 | bytes 10000000 | tf_op jit(solution)/shard_map/compressed_step/pallas_call | solution.py:511
  159.6 0.0 copy-start
  159.6 1.7 copy-done
  161.2 0.0 copy-start.1
  161.2 0.9 copy-done.1
  162.1 0.0 copy-start.2
  162.1 0.9 copy-done.2
  163.0 2.9 %feedback.1 = (f32[576,1024]{1,0:T(8,128)}, f32[32,576]{1,0:T(8,128)}) custom-call(f32[576,1024]{1,0:T(8,128)S(1)} %copy-done, f32[8,4,576]{2,1,0:T(4,128)S(1)} %copy-done.2, f32[8,32,128]{2,1,0:T(8,128)S(1)} %copy-done.1), custom_call_target="tpu_custom_call" | custom-call | tf_op jit(solution)/shard_map/feedback/pallas_call | solution.py:584
Async XLA Ops:
  159.6 1.7 %copy-start = (f32[576,1024]{1,0:T(8,128)S(1)}, f32[576,1024]{1,0:T(8,128)}, u32[]{:S(2)}) copy-start(f32[576,1024]{1,0:T(8,128)} %get-tuple-element.7.memory) | copy-start | bytes 7077892
  161.2 0.9 copy-start.1
  162.1 0.9 copy-start.2

commit v3 on v2

--- a/solution.py
+++ b/solution.py
@@ -12,7 +12,9 @@
 CHUNKS = 8
 COLS = 128
 TAPS = 9
+T_AT = 1
 P_AT = 2
+EARLY = 3
 
 
 def sp_at(x, z):
@@ -272,18 +274,18 @@
     def t_band(which):
         acc = None
         for a in range(3):
-            for b in range(3):
-                at = pl.ds(pl.multiple_of(which * band + a * width, width), band)
-                term = jnp.dot(q_flip[a * 3 + b], taps[b, :, at], preferred_element_type=jnp.float32)
-                acc = term if acc is None else acc + term
+            at = pl.ds(pl.multiple_of(which * band + a * width, width), band)
+            stacked = taps[:, :, at].reshape(3 * RING * share, band)
+            term = jnp.dot(q_flip[a], stacked, preferred_element_type=jnp.float32)
+            acc = term if acc is None else acc + term
         t_term[which] = acc[:rank] + (acc[rank : 2 * rank] + acc[2 * rank : 3 * rank])
 
     def t_start():
         own_q.wait()
         for step in (1, 3, 2):
             q_in(step).wait_recv()
-        for tap in range(TAPS):
-            q_flip[tap] = q_near[tap].reshape(RING * share, lanes).T
+        for a in range(3):
+            q_flip[a] = q_near[3 * a : 3 * a + 3].reshape(3 * RING * share, lanes).T
 
     def t_bands(first):
         def one(i, carry):
@@ -339,10 +341,8 @@
     def orthogonal():
         for d in range(1, count_sp):
             p_gather_in(d).wait_recv()
-        gram = jnp.zeros((rank, rank), jnp.float32)
-        for j in range(CHUNKS):
-            block = p_chunk(j)
-            gram = gram + exact_dot(block, block, ((1,), (1,)))
+        p_total = jnp.concatenate([p_chunk(j) for j in range(CHUNKS)], axis=1)
+        gram = exact_dot(p_total, p_total, ((1,), (1,)))
         row_at = lax.broadcasted_iota(jnp.int32, (rank, rank), 0)
         col_at = lax.broadcasted_iota(jnp.int32, (rank, rank), 1)
         work[:, :rank] = gram
@@ -365,12 +365,71 @@
 
         lax.fori_loop(0, rank, eliminate, 0)
         lower_inverse = jnp.where(col_at <= row_at, work[:, rank : 2 * rank], 0.0)
+        whole = exact_dot(lower_inverse, p_total, ((1,), (0,)))
         for j in range(CHUNKS):
-            p_ortho[j] = exact_dot(lower_inverse, p_chunk(j), ((1,), (0,)))
+            p_ortho[j] = whole[:, j * COLS : (j + 1) * COLS]
         q_sum[...] = jnp.zeros_like(q_sum)
 
     def add_q(k):
-        q_sum[...] = q_sum[...] + exact_dot(p_ortho[k], total[k], ((1,), (1,)))
+        m0, m1, m2 = split(total[k])
+        p0, p1, p2 = split(p_ortho[k])
+        m_side = jnp.concatenate([m0, m0, m0, m1, m1, m2], axis=1)
+        p_side = jnp.concatenate([p0, p1, p2, p0, p1, p0], axis=1).T
+        q_sum[:, :rank] = q_sum[:, :rank] + jnp.dot(m_side, p_side, preferred_element_type=jnp.float32)
+
+    def multiply(first, count):
+        depth = gbuf.shape[1]
+        per_side = part.shape[4]
+
+        def one(a, carry):
+            at = pl.ds(pl.multiple_of(a * width, width), depth)
+            stacked = taps[:, :, at].reshape(3 * RING * share, depth)
+            chosen = gbuf[first] if count == 1 else jnp.concatenate([gbuf[first], gbuf[first + 1]], axis=1)
+            product = jnp.dot(stacked, chosen, preferred_element_type=jnp.float32)
+            for c in range(count):
+                for b in range(3):
+                    for owner in range(RING):
+                        for side in range(2):
+                            line = b * RING * share + (owner * 2 + side) * per_side
+                            part[first + c, owner, side, a * 3 + b] = product[
+                                line : line + per_side, c * COLS : (c + 1) * COLS
+                            ]
+                far(first + c, 0, a).start()
+                far(first + c, 1, a).start()
+            return carry
+
+        lax.fori_loop(0, 3, one, 0)
+
+    def pass_on(k):
+        for group in range(3):
+            some = pl.ds(group * 3, 3)
+            far(k, 0, group).wait_recv()
+            part[k, x_right, 0, some] = part[k, x_right, 0, some] + relay[k, 0, some]
+            near(k, 0, group).start()
+            far(k, 1, group).wait_recv()
+            part[k, x_left, 1, some] = part[k, x_left, 1, some] + relay[k, 1, some]
+            near(k, 1, group).start()
+
+    def complete(k, with_q):
+        for group in range(3):
+            near(k, 0, group).wait_recv()
+            near(k, 1, group).wait_recv()
+        count = part.shape[4]
+        for side in range(2):
+            for tap in range(TAPS):
+                at = pl.ds(side * count * TAPS + tap, count, stride=TAPS)
+                total[k, at, :] = (
+                    total[k, at, :] + part[k, x, side, tap] + (piece[k, 0, side, tap] + piece[k, 1, side, tap])
+                )
+        mem_out(k).start()
+        pl.when(with_q)(lambda: add_q(k))
+
+    def over(first, count, body):
+        def one(i, carry):
+            body(first + i)
+            return carry
+
+        lax.fori_loop(0, count, one, 0)
 
     def step(j, carry):
         @pl.when(j + 3 < CHUNKS)
@@ -385,39 +444,19 @@
         def _():
             forward_in(j, 0).wait_recv()
             forward_in(j, 1).wait_recv()
-            depth = gbuf.shape[1]
-            for a in range(3):
-                for b in range(3):
-                    product = jnp.dot(
-                        taps[b, :, a * width : a * width + depth], gbuf[j], preferred_element_type=jnp.float32
-                    )
-                    count = part.shape[4]
-                    for owner in range(RING):
-                        for side in range(2):
-                            first = (owner * 2 + side) * count
-                            part[j, owner, side, a * 3 + b] = product[first : first + count]
-                far(j, 0, a).start()
-                far(j, 1, a).start()
-
-        @pl.when((j >= 1) & (j <= CHUNKS))
-        def _():
-            k = j - 1
-            for group in range(3):
-                some = pl.ds(group * 3, 3)
-                far(k, 0, group).wait_recv()
-                part[k, x_right, 0, some] = part[k, x_right, 0, some] + relay[k, 0, some]
-                near(k, 0, group).start()
-                far(k, 1, group).wait_recv()
-                part[k, x_left, 1, some] = part[k, x_left, 1, some] + relay[k, 1, some]
-                near(k, 1, group).start()
-
-        @pl.when(j == 0)
+
+        alone = (j == 0) | (j == CHUNKS - 1)
+        paired = (j > 0) & (j < CHUNKS - 1) & (lax.rem(j, 2) == 0)
+        pl.when(alone)(lambda: multiply(j, 1))
+        pl.when(paired)(lambda: multiply(j - 1, 2))
+
+        pl.when((j == 1) | (j == CHUNKS))(lambda: pass_on(j - 1))
+        pl.when((j > 1) & (j < CHUNKS) & (lax.rem(j, 2) == 1))(lambda: over(j - 2, 2, pass_on))
+
+        @pl.when(j == T_AT)
         def _():
             t_start()
             t_bands(0)
-
-        @pl.when(j == 1)
-        def _():
             t_bands(RING // 2)
             t_finish()
 
@@ -425,39 +464,22 @@
         pl.when(j == P_AT + 1)(p_sum_sp)
         pl.when(j == P_AT + 2)(p_sum_rep)
         pl.when(j == P_AT + 3)(orthogonal)
-
-        @pl.when(j >= 2)
-        def _():
-            k = j - 2
-            for group in range(3):
-                near(k, 0, group).wait_recv()
-                near(k, 1, group).wait_recv()
-            count = part.shape[4]
-            for side in range(2):
-                for tap in range(TAPS):
-                    at = pl.ds(side * count * TAPS + tap, count, stride=TAPS)
-                    total[k, at, :] = (
-                        total[k, at, :] + part[k, x, side, tap] + (piece[k, 0, side, tap] + piece[k, 1, side, tap])
-                    )
-
-            mem_out(k).start()
-
-            @pl.when(j >= P_AT + 3)
-            def _():
-                add_q(k)
-
-        @pl.when(j == P_AT + 3)
-        def _():
-            for k in range(P_AT + 1):
-                add_q(k)
+        ready = j >= P_AT + 3
+
+        pl.when((j == 2) | (j == CHUNKS + 1))(lambda: complete(lax.select(j == 2, 0, CHUNKS - 1), ready))
+        pl.when((j > 2) & (j <= CHUNKS) & (lax.rem(j, 2) == 0))(
+            lambda: over(j - 3, 2, lambda k: complete(k, ready))
+        )
+        pl.when(j == P_AT + 3)(lambda: over(0, EARLY, add_q))
 
         return carry
 
     lax.fori_loop(0, CHUNKS + 2, step, 0)
 
     lines = rank // count_rep
+    q_lines = q_sum[...].T
     for i in range(count_rep):
-        q_src[i] = q_sum[i * lines : (i + 1) * lines]
+        q_src[i] = q_lines[i * lines : (i + 1) * lines]
     for d in range(1, count_rep):
         q_scatter(d).start()
     acc = q_src[rep]
@@ -531,7 +553,7 @@
             pltpu.VMEM((CHUNKS, 2, 2, TAPS, per_side, COLS), f32),
             pltpu.VMEM((CHUNKS, rows, COLS), f32),
             pltpu.VMEM((TAPS, RING, share, 128), bf16),
-            pltpu.VMEM((TAPS, 128, RING * share), bf16),
+            pltpu.VMEM((3, 128, 3 * RING * share), bf16),
             pltpu.VMEM((RING, rank, band), f32),
             pltpu.VMEM((RING - 1, rank, band), f32),
             pltpu.VMEM((count_sp, *p_block), f32),
@@ -542,7 +564,7 @@
             pltpu.VMEM((rank, 128), f32),
             pltpu.VMEM((count_rep, *q_block), f32),
             pltpu.VMEM((count_rep - 1, *q_block), f32),
-            pltpu.VMEM((rank, rows), f32),
+            pltpu.VMEM((rows, 128), f32),
             dma((chans // COLS,)), dma((3,)), dma((3,)), dma, dma((2,)), dma((2,)), dma((CHUNKS,)), dma((CHUNKS,)),
             two, two, two, two, three, three, three, three, dma((CHUNKS,)),
             dma((3,)), dma((3,)), dma, dma((3,)), dma((3,)),
@@ -592,7 +614,7 @@
         ],
         out_specs=(pl.BlockSpec(block, lambda i: (0, i)), pl.BlockSpec((rank, rows), lambda i: (0, 0))),
         scratch_shapes=[pltpu.VMEM((rows, 6 * rank), jnp.bfloat16)],
-        compiler_params=pltpu.CompilerParams(vmem_limit_bytes=32 * 1024 * 1024),
+        compiler_params=pltpu.CompilerParams(vmem_limit_bytes=60 * 1024 * 1024),
         name="feedback",
     )(memory, q_parts, p_ortho)
 

time: 166 us -> 167 us (level)
  Pallas kernels: 162 us -> 166 us
  local copies, waits for them, and re-layouts: 3.45 us -> 0 us
    unnamed x6 -> x0, local copies, waits for them, and re-layouts: 3.45 us -> none
    pallas_call x1, Pallas kernels: 159 us -> 161 us  [compressed_step(): pl.pallas_call(functools.partial(step_kernel, count_rep), out_shape=(jax....]
    pallas_call x1, Pallas kernels: 2.87 us -> 4.62 us  [feedback(): pl.pallas_call(feedback_kernel, grid=(chans // block[1],), out_shape=(jax...]
where the time goes in v3:
time: 167 us
  Pallas kernels  166 us (99%)
    pallas_call x1, Pallas kernels, compressed_step(): pl.pallas_call(functools.partial(step_kernel, count_rep), out_shape=(jax....  161 us
    pallas_call x1, Pallas kernels, feedback(): pl.pallas_call(feedback_kernel, grid=(chans // block[1],), out_shape=(jax...  4.62 us

profile of v3, /device:TPU:1, one launch (start us, length us, event | category | flops | bytes accessed | tf_op | source)
XLA Modules:
  0.0 166.7 jit_solution(5950501503214092691)
XLA Ops:
  0.6 161.4 %compressed_step.1 = (f32[576,1024]{1,0:T(8,128)}, f32[8,4,576]{2,1,0:T(4,128)}, f32[8,32,128]{2,1,0:T(8,128)}) custom-call(bf16[1024,1024]{1,0:T(8,128)(2,1)} %bitcast.6, bf16[1024,1024]{1,0:T(8,128)(2,1)} %bitcast.7, f32[576,1024]{1,0:T(8,128)} %bitcast.4, f32[32,576]{1,0:T(8,128)} %q_own.1), custom_call_target="tpu_custom_call" | custom-call | flops 19327352832 | bytes 10000000 | tf_op jit(solution)/shard_map/compressed_step/pallas_call | solution.py:533
  162.1 4.6 %feedback.1 = (f32[576,1024]{1,0:T(8,128)}, f32[32,576]{1,0:T(8,128)}) custom-call(f32[576,1024]{1,0:T(8,128)} %get-tuple-element.7.memory, f32[8,4,576]{2,1,0:T(4,128)} %get-tuple-element.8.q_parts, f32[8,32,128]{2,1,0:T(8,128)} %get-tuple-element.9.p_ortho), custom_call_target="tpu_custom_call" | custom-call | tf_op jit(solution)/shard_map/feedback/pallas_call | solution.py:606

commit v4 on v3

--- a/solution.py
+++ b/solution.py
@@ -12,9 +12,9 @@
 CHUNKS = 8
 COLS = 128
 TAPS = 9
-T_AT = 1
-P_AT = 2
-EARLY = 3
+T_AT = 0
+P_AT = (2, 4, 5, 7)
+EARLY = 5
 
 
 def sp_at(x, z):
@@ -89,16 +89,12 @@
         return pltpu.make_async_copy(g.at[:, columns(j)], gbuf.at[j, slot(z, 0, band)], g_own.at[j])
 
     def direct(j, side):
-        return remote(
-            g.at[:, columns(j)], gbuf.at[j, slot(z, 0, band)], d_send.at[j, side], d_recv.at[j, side],
-            up if side == 0 else down,
-        )
+        ref = gbuf.at[j, slot(z, 0, band)]
+        return remote(ref, ref, d_send.at[j, side], d_recv.at[j, side], up if side == 0 else down)
 
     def direct_in(j, side):
-        return remote(
-            g.at[:, columns(j)], gbuf.at[j, slot(z_down if side == 0 else z_up, 0, band)],
-            d_send.at[j, side], d_recv.at[j, side], up,
-        )
+        ref = gbuf.at[j, slot(z_down if side == 0 else z_up, 0, band)]
+        return remote(ref, ref, d_send.at[j, side], d_recv.at[j, side], up)
 
     def forward(j, side):
         ref = gbuf.at[j, slot(z_down if side == 0 else z_up, side * half, half)]
@@ -179,24 +175,33 @@
 
     pairs = frames.shape[1] // COLS
     owners = COLS // share
+    own_grad(0).start()
     for i in range(pairs):
         column_in(i).start()
     pl.semaphore_wait(barrier, count_sp + count_rep - 2)
+    own_grad(0).wait()
     direct(0, 0).start()
     direct(0, 1).start()
 
-    for i in range(pairs):
-        column_in(i).wait()
-        turned = local[i].T
-        for k in range(owners):
-            owner = i * owners + k
-            flipped[owner // RING, owner % RING] = turned[k * share : (k + 1) * share]
-    for step in (1, 3, 2):
-        frames_out(step).start()
+    per_x = RING // owners
+    for first in range(per_x):
+        for i in range(first, pairs, per_x):
+            column_in(i).wait()
+            turned = local[i].T
+            for k in range(owners):
+                owner = i * owners + k
+                flipped[owner // RING, owner % RING] = turned[k * share : (k + 1) * share]
+        for target in range(first * owners, (first + 1) * owners):
+            away = lax.rem(target - z + RING, RING)
+
+            @pl.when(away != 0)
+            def _(away=away):
+                frames_out(away).start()
     own_frames = pltpu.make_async_copy(flipped.at[:, z], raw.at[z], f_own)
     own_frames.start()
     for j in range(CHUNKS):
         err_in(j).start()
+    for j in range(1, CHUNKS):
         own_grad(j).start()
 
     thirds = [third.astype(jnp.float32) for third in split(q_own[...])]
@@ -236,9 +241,11 @@
         for side in range(2):
             direct(j, side).start()
 
-    start_forward(0)
     own_frames.wait()
     place_band(z)
+    start_forward(0)
+    for j in range(1, CHUNKS):
+        own_grad(j).wait()
 
     for j in range(CHUNKS):
         err_in(j).wait()
@@ -252,7 +259,6 @@
     place_band(z_down)
     place_band(z_up)
     frames_in(2).wait_recv()
-    start_direct(2)
 
     bottom = raw.at[RING - 1, :, :, band - width : band]
     above = remote(bottom, halo.at[0], h_send.at[0], h_recv.at[0], right)
@@ -267,10 +273,6 @@
     place(0, jnp.where(x == 0, zero, halo[0].reshape(RING * share, width)))
     place(rows + 1, jnp.where(x == RING - 1, zero, halo[1].reshape(RING * share, width)))
 
-    start_forward(1)
-    for j in range(CHUNKS):
-        own_grad(j).wait()
-
     def t_band(which):
         acc = None
         for a in range(3):
@@ -377,7 +379,7 @@
         p_side = jnp.concatenate([p0, p1, p2, p0, p1, p0], axis=1).T
         q_sum[:, :rank] = q_sum[:, :rank] + jnp.dot(m_side, p_side, preferred_element_type=jnp.float32)
 
-    def multiply(first, count):
+    def multiply(first, count, after):
         depth = gbuf.shape[1]
         per_side = part.shape[4]
 
@@ -396,6 +398,11 @@
                             ]
                 far(first + c, 0, a).start()
                 far(first + c, 1, a).start()
+
+            @pl.when((a == 0) & (after < CHUNKS))
+            def _():
+                start_forward(after)
+
             return carry
 
         lax.fori_loop(0, 3, one, 0)
@@ -432,13 +439,9 @@
         lax.fori_loop(0, count, one, 0)
 
     def step(j, carry):
-        @pl.when(j + 3 < CHUNKS)
-        def _():
-            start_direct(j + 3)
-
         @pl.when(j + 2 < CHUNKS)
         def _():
-            start_forward(j + 2)
+            start_direct(j + 2)
 
         @pl.when(j < CHUNKS)
         def _():
@@ -446,12 +449,13 @@
             forward_in(j, 1).wait_recv()
 
         alone = (j == 0) | (j == CHUNKS - 1)
-        paired = (j > 0) & (j < CHUNKS - 1) & (lax.rem(j, 2) == 0)
-        pl.when(alone)(lambda: multiply(j, 1))
-        pl.when(paired)(lambda: multiply(j - 1, 2))
+        even = lax.rem(j, 2) == 0
+        pl.when(alone)(lambda: multiply(j, 1, j + 1))
+        pl.when((j > 0) & (j < CHUNKS - 1) & even)(lambda: multiply(j - 1, 2, j + 1))
+        pl.when((j < CHUNKS - 1) & jnp.logical_not(even))(lambda: start_forward(j + 1))
 
         pl.when((j == 1) | (j == CHUNKS))(lambda: pass_on(j - 1))
-        pl.when((j > 1) & (j < CHUNKS) & (lax.rem(j, 2) == 1))(lambda: over(j - 2, 2, pass_on))
+        pl.when((j > 1) & (j < CHUNKS) & jnp.logical_not(even))(lambda: over(j - 2, 2, pass_on))
 
         @pl.when(j == T_AT)
         def _():
@@ -460,17 +464,15 @@
             t_bands(RING // 2)
             t_finish()
 
-        pl.when(j == P_AT)(p_terms)
-        pl.when(j == P_AT + 1)(p_sum_sp)
-        pl.when(j == P_AT + 2)(p_sum_rep)
-        pl.when(j == P_AT + 3)(orthogonal)
-        ready = j >= P_AT + 3
+        for at, stage in zip(P_AT, (p_terms, p_sum_sp, p_sum_rep, orthogonal)):
+            pl.when(j == at)(stage)
+        ready = j >= P_AT[-1]
 
         pl.when((j == 2) | (j == CHUNKS + 1))(lambda: complete(lax.select(j == 2, 0, CHUNKS - 1), ready))
-        pl.when((j > 2) & (j <= CHUNKS) & (lax.rem(j, 2) == 0))(
+        pl.when((j > 2) & (j <= CHUNKS) & even)(
             lambda: over(j - 3, 2, lambda k: complete(k, ready))
         )
-        pl.when(j == P_AT + 3)(lambda: over(0, EARLY, add_q))
+        pl.when(j == P_AT[-1])(lambda: over(0, EARLY, add_q))
 
         return carry
 

time: 167 us -> 162 us (0.970)
  Pallas kernels: 166 us -> 161 us
    pallas_call x1, Pallas kernels: 161 us -> 157 us  [compressed_step(): pl.pallas_call(functools.partial(step_kernel, count_rep), out_shape=(jax....]
where the time goes in v4:
time: 162 us
  Pallas kernels  161 us (99%)
    pallas_call x1, Pallas kernels, compressed_step(): pl.pallas_call(functools.partial(step_kernel, count_rep), out_shape=(jax....  157 us
    pallas_call x1, Pallas kernels, feedback(): pl.pallas_call(feedback_kernel, grid=(chans // block[1],), out_shape=(jax...  4.61 us

profile of v4, /device:TPU:1, one launch (start us, length us, event | category | flops | bytes accessed | tf_op | source)
XLA Modules:
  0.0 161.8 jit_solution(8589227255710886068)
XLA Ops:
  0.6 156.5 %compressed_step.1 = (f32[576,1024]{1,0:T(8,128)}, f32[8,4,576]{2,1,0:T(4,128)}, f32[8,32,128]{2,1,0:T(8,128)}) custom-call(bf16[1024,1024]{1,0:T(8,128)(2,1)} %bitcast.6, bf16[1024,1024]{1,0:T(8,128)(2,1)} %bitcast.7, f32[576,1024]{1,0:T(8,128)} %bitcast.4, f32[32,576]{1,0:T(8,128)} %q_own.1), custom_call_target="tpu_custom_call" | custom-call | flops 19327352832 | bytes 10000000 | tf_op jit(solution)/shard_map/compressed_step/pallas_call | solution.py:535
  157.2 4.6 %feedback.1 = (f32[576,1024]{1,0:T(8,128)}, f32[32,576]{1,0:T(8,128)}) custom-call(f32[576,1024]{1,0:T(8,128)} %get-tuple-element.7.memory, f32[8,4,576]{2,1,0:T(4,128)} %get-tuple-element.8.q_parts, f32[8,32,128]{2,1,0:T(8,128)} %get-tuple-element.9.p_ortho), custom_call_target="tpu_custom_call" | custom-call | tf_op jit(solution)/shard_map/feedback/pallas_call | solution.py:608

commit v5 on v4

--- a/solution.py
+++ b/solution.py
@@ -43,7 +43,7 @@
 
 def step_kernel(
     count_rep, frames, g, err, q_own, memory, q_next, p_ortho,
-    local, q_turned, q_taps, flipped, raw, halo, taps, gbuf, part, relay, piece, total,
+    local, f_relay, t_relay, q_turned, q_taps, flipped, raw, halo, taps, gbuf, part, relay, piece, total,
     q_near, q_flip, t_term, t_near, p_src, p_near, p_one, p_far, p_all, work, q_src, q_got, q_sum,
     l_in, f_send, f_recv, f_own, h_send, h_recv, e_in, g_own,
     d_send, d_recv, r_send, r_recv, a_send, a_recv, b_send, b_recv, out_sem,
@@ -68,16 +68,31 @@
     def at_rep(d):
         return {"rep": lax.rem(rep + d, count_rep)}
 
-    def frames_out(step):
+    near_z, far_z = (z_up, z_down), lax.rem(z + 2, RING)
+    towards = (up, down)
+    some_x = RING // 2
+
+    def frames_near(side):
+        return remote(flipped.at[:, near_z[side]], raw.at[z], f_send.at[side], f_recv.at[side], towards[side])
+
+    def frames_near_in(side):
+        return remote(flipped.at[:, z], raw.at[near_z[1 - side]], f_send.at[side], f_recv.at[side], up)
+
+    def frames_far(side):
+        part_x = pl.ds(side * some_x, some_x)
         return remote(
-            flipped.at[:, lax.rem(z + step, RING)], raw.at[z], f_send.at[step - 1], f_recv.at[step - 1],
-            sp_at(x, z + step),
+            flipped.at[part_x, far_z], f_relay.at[side], f_send.at[2 + side], f_recv.at[2 + side], towards[side]
         )
 
-    def frames_in(step):
+    def frames_on(side):
+        part_x = pl.ds(side * some_x, some_x)
         return remote(
-            flipped.at[:, z], raw.at[lax.rem(z + RING - step, RING)], f_send.at[step - 1], f_recv.at[step - 1], up
+            f_relay.at[side], raw.at[near_z[1 - side], part_x], f_send.at[4 + side], f_recv.at[4 + side], towards[side]
         )
+
+    def frames_far_in(side):
+        part_x = pl.ds(side * some_x, some_x)
+        return remote(f_relay.at[side], raw.at[far_z, part_x], f_send.at[4 + side], f_recv.at[4 + side], up)
 
     def columns(j):
         return pl.ds(pl.multiple_of(j * COLS, COLS), COLS)
@@ -131,10 +146,13 @@
         source = lax.rem(x + RING - step, RING)
         return remote(q_taps, q_near.at[:, source], q_send.at[step - 1], q_recv.at[step - 1], right)
 
-    def t_out(step):
+    def t_far(side):
+        some = pl.ds(side * (rank // 2), rank // 2)
+        return remote(t_term.at[far_z, some], t_relay.at[side], t_send.at[side], t_recv.at[side], towards[side])
+
+    def t_out(side):
         return remote(
-            t_term.at[lax.rem(z + step, RING)], t_near.at[step - 1], t_send.at[step - 1], t_recv.at[step - 1],
-            sp_at(x, z + step),
+            t_term.at[near_z[side]], t_near.at[side], t_send.at[2 + side], t_recv.at[2 + side], towards[side]
         )
 
     def p_scatter(d):
@@ -191,12 +209,10 @@
             for k in range(owners):
                 owner = i * owners + k
                 flipped[owner // RING, owner % RING] = turned[k * share : (k + 1) * share]
-        for target in range(first * owners, (first + 1) * owners):
-            away = lax.rem(target - z + RING, RING)
-
-            @pl.when(away != 0)
-            def _(away=away):
-                frames_out(away).start()
+    for side in range(2):
+        frames_far(side).start()
+    for side in range(2):
+        frames_near(side).start()
     own_frames = pltpu.make_async_copy(flipped.at[:, z], raw.at[z], f_own)
     own_frames.start()
     for j in range(CHUNKS):
@@ -253,12 +269,16 @@
         for h in range(2):
             p_src[2 * j + h] = term[h * (rank // 2) : (h + 1) * (rank // 2)]
 
-    frames_in(1).wait_recv()
-    frames_in(3).wait_recv()
+    for side in range(2):
+        frames_far(side).wait_recv()
+        frames_on(side).start()
+    for side in range(2):
+        frames_near_in(side).wait_recv()
     start_direct(1)
     place_band(z_down)
     place_band(z_up)
-    frames_in(2).wait_recv()
+    for side in range(2):
+        frames_far_in(side).wait_recv()
 
     bottom = raw.at[RING - 1, :, :, band - width : band]
     above = remote(bottom, halo.at[0], h_send.at[0], h_recv.at[0], right)
@@ -297,13 +317,20 @@
         lax.fori_loop(0, RING // 2, one, 0)
 
     def t_finish():
-        for step in (1, 3, 2):
-            t_out(step).start()
+        for side in range(2):
+            t_far(side).start()
+
+    def t_pass_on():
+        for side in range(2):
+            some = pl.ds(side * (rank // 2), rank // 2)
+            t_far(side).wait_recv()
+            t_term[near_z[side], some] = t_term[near_z[side], some] + t_relay[side]
+            t_out(side).start()
 
     def p_terms():
-        for step in (1, 3, 2):
-            t_out(step).wait_recv()
-        full = t_term[z] + (t_near[0] + t_near[1] + t_near[2])
+        for side in range(2):
+            t_out(side).wait_recv()
+        full = t_term[z] + (t_near[0] + t_near[1])
         parts = jnp.concatenate(split(full), axis=0)
 
         def add(j, carry):
@@ -464,6 +491,7 @@
             t_bands(RING // 2)
             t_finish()
 
+        pl.when(j == T_AT + 1)(t_pass_on)
         for at, stage in zip(P_AT, (p_terms, p_sum_sp, p_sum_rep, orthogonal)):
             pl.when(j == at)(stage)
         ready = j >= P_AT[-1]
@@ -505,10 +533,14 @@
         return carry
 
     lax.fori_loop(0, CHUNKS, finish, 0)
+    for side in range(2):
+        frames_near(side).wait_send()
+        frames_far(side).wait_send()
+        frames_on(side).wait_send()
+        t_far(side).wait_send()
+        t_out(side).wait_send()
     for step_ in (1, 3, 2):
-        frames_out(step_).wait_send()
         q_out(step_).wait_send()
-        t_out(step_).wait_send()
     for d in range(1, count_sp):
         p_scatter(d).wait_send()
         p_gather(d).wait_send()
@@ -543,6 +575,8 @@
         out_specs=(any_spec, vmem_spec, vmem_spec),
         scratch_shapes=[
             pltpu.VMEM((chans // COLS, band, COLS), bf16),
+            pltpu.VMEM((2, RING // 2, share, band), bf16),
+            pltpu.VMEM((2, rank // 2, band), f32),
             pltpu.VMEM((rows, 128), f32),
             pltpu.VMEM((TAPS, share, 128), bf16),
             pltpu.VMEM((RING, RING, share, band), bf16),
@@ -557,7 +591,7 @@
             pltpu.VMEM((TAPS, RING, share, 128), bf16),
             pltpu.VMEM((3, 128, 3 * RING * share), bf16),
             pltpu.VMEM((RING, rank, band), f32),
-            pltpu.VMEM((RING - 1, rank, band), f32),
+            pltpu.VMEM((2, rank, band), f32),
             pltpu.VMEM((count_sp, *p_block), f32),
             pltpu.VMEM((count_sp - 1, *p_block), f32),
             pltpu.VMEM(p_block, f32),
@@ -567,9 +601,9 @@
             pltpu.VMEM((count_rep, *q_block), f32),
             pltpu.VMEM((count_rep - 1, *q_block), f32),
             pltpu.VMEM((rows, 128), f32),
-            dma((chans // COLS,)), dma((3,)), dma((3,)), dma, dma((2,)), dma((2,)), dma((CHUNKS,)), dma((CHUNKS,)),
+            dma((chans // COLS,)), dma((6,)), dma((6,)), dma, dma((2,)), dma((2,)), dma((CHUNKS,)), dma((CHUNKS,)),
             two, two, two, two, three, three, three, three, dma((CHUNKS,)),
-            dma((3,)), dma((3,)), dma, dma((3,)), dma((3,)),
+            dma((3,)), dma((3,)), dma, dma((4,)), dma((4,)),
             dma((count_sp - 1,)), dma((count_sp - 1,)), dma((count_rep - 1,)), dma((count_rep - 1,)),
             dma((count_sp - 1,)), dma((count_sp - 1,)), dma((count_rep - 1,)), dma((count_rep - 1,)),
             dma((count_rep - 1,)), dma((count_rep - 1,)),

time: 162 us -> 160 us (0.988)
  Pallas kernels: 161 us -> 159 us
    pallas_call x1, Pallas kernels: 157 us -> 154 us  [compressed_step(): pl.pallas_call(functools.partial(step_kernel, count_rep), out_shape=(jax....]
where the time goes in v5:
time: 160 us; the launch traced here: 159 us
  Pallas kernels  159 us (99%)
    pallas_call x1, Pallas kernels, compressed_step(): pl.pallas_call(functools.partial(step_kernel, count_rep), out_shape=(jax....  154 us
    pallas_call x1, Pallas kernels, feedback(): pl.pallas_call(feedback_kernel, grid=(chans // block[1],), out_shape=(jax...  4.62 us

profile of v5, /device:TPU:1, one launch (start us, length us, event | category | flops | bytes accessed | tf_op | source)
XLA Modules:
  0.0 159.3 jit_solution(4639578457244106495)
XLA Ops:
  0.6 154.0 %compressed_step.1 = (f32[576,1024]{1,0:T(8,128)}, f32[8,4,576]{2,1,0:T(4,128)}, f32[8,32,128]{2,1,0:T(8,128)}) custom-call(bf16[1024,1024]{1,0:T(8,128)(2,1)} %bitcast.6, bf16[1024,1024]{1,0:T(8,128)(2,1)} %bitcast.7, f32[576,1024]{1,0:T(8,128)} %bitcast.4, f32[32,576]{1,0:T(8,128)} %q_own.1), custom_call_target="tpu_custom_call" | custom-call | flops 19327352832 | bytes 10000000 | tf_op jit(solution)/shard_map/compressed_step/pallas_call | solution.py:567
  154.7 4.6 %feedback.1 = (f32[576,1024]{1,0:T(8,128)}, f32[32,576]{1,0:T(8,128)}) custom-call(f32[576,1024]{1,0:T(8,128)} %get-tuple-element.7.memory, f32[8,4,576]{2,1,0:T(4,128)} %get-tuple-element.8.q_parts, f32[8,32,128]{2,1,0:T(8,128)} %get-tuple-element.9.p_ortho), custom_call_target="tpu_custom_call" | custom-call | tf_op jit(solution)/shard_map/feedback/pallas_call | solution.py:642

commit v6 on v5

--- a/solution.py
+++ b/solution.py
@@ -13,8 +13,8 @@
 COLS = 128
 TAPS = 9
 T_AT = 0
-P_AT = (2, 4, 5, 7)
-EARLY = 5
+P_AT = (2, 3, 4, 5)
+EARLY = 3
 
 
 def sp_at(x, z):
@@ -42,12 +42,12 @@
 
 
 def step_kernel(
-    count_rep, frames, g, err, q_own, memory, q_next, p_ortho,
+    count_rep, frames, g, err, q_own, memory, q_next, p_side,
     local, f_relay, t_relay, q_turned, q_taps, flipped, raw, halo, taps, gbuf, part, relay, piece, total,
-    q_near, q_flip, t_term, t_near, p_src, p_near, p_one, p_far, p_all, work, q_src, q_got, q_sum,
+    q_near, q_flip, t_term, t_near, p_src, p_near, p_one, p_far, p_all, work, q_src, q_got, q_sum, x_term, x_got,
     l_in, f_send, f_recv, f_own, h_send, h_recv, e_in, g_own,
     d_send, d_recv, r_send, r_recv, a_send, a_recv, b_send, b_recv, out_sem,
-    q_send, q_recv, q_copy, t_send, t_recv, s1, r1, s2, r2, s3, r3, s4, r4, s5, r5,
+    q_send, q_recv, q_copy, t_send, t_recv, s1, r1, s2, r2, s3, r3, s4, r4, s5, r5, x_send, x_recv,
 ):
     sp, rep = lax.axis_index("sp"), lax.axis_index("rep")
     x, z = sp // RING, lax.rem(sp, RING)
@@ -171,6 +171,9 @@
     def p_gather_in(d):
         ref = p_all.at[lax.rem(sp + count_sp - d, count_sp)]
         return remote(ref, ref, s3.at[d - 1], r3.at[d - 1], at_sp(d))
+
+    def x_out(step):
+        return remote(x_term.at[step - 1], x_got.at[step - 1], x_send.at[step - 1], x_recv.at[step - 1], sp_at(x + step, z))
 
     def q_scatter(d):
         return remote(q_src.at[lax.rem(rep + d, count_rep)], q_got.at[d - 1], s4.at[d - 1], r4.at[d - 1], at_rep(d))
@@ -395,16 +398,47 @@
         lax.fori_loop(0, rank, eliminate, 0)
         lower_inverse = jnp.where(col_at <= row_at, work[:, rank : 2 * rank], 0.0)
         whole = exact_dot(lower_inverse, p_total, ((1,), (0,)))
-        for j in range(CHUNKS):
-            p_ortho[j] = whole[:, j * COLS : (j + 1) * COLS]
+        p0, p1, p2 = split(whole)
+        p_side[...] = jnp.concatenate([p0, p1, p2, p0, p1, p0], axis=0)
         q_sum[...] = jnp.zeros_like(q_sum)
 
+    def by_p(rows_of, k):
+        m0, m1, m2 = split(rows_of)
+        m_side = jnp.concatenate([m0, m0, m0, m1, m1, m2], axis=1)
+        across = jnp.concatenate([p_side[i * rank : (i + 1) * rank, columns(k)] for i in range(6)], axis=1)
+        return jnp.dot(m_side, across.T, preferred_element_type=jnp.float32)
+
     def add_q(k):
-        m0, m1, m2 = split(total[k])
-        p0, p1, p2 = split(p_ortho[k])
-        m_side = jnp.concatenate([m0, m0, m0, m1, m1, m2], axis=1)
-        p_side = jnp.concatenate([p0, p1, p2, p0, p1, p0], axis=1).T
-        q_sum[:, :rank] = q_sum[:, :rank] + jnp.dot(m_side, p_side, preferred_element_type=jnp.float32)
+        q_sum[:, :rank] = q_sum[:, :rank] + by_p(total[k], k)
+
+    last = CHUNKS - 1
+
+    def last_terms():
+        for step in (1, 3, 2):
+            owner = lax.rem(x + step, RING)
+            terms = by_p(part[last, owner].reshape(q_sum.shape[0], COLS), last)
+            x_term[step - 1] = terms.T
+            x_out(step).start()
+
+    def last_own():
+        count = part.shape[4]
+        for side in range(2):
+            for tap in range(TAPS):
+                at = pl.ds(side * count * TAPS + tap, count, stride=TAPS)
+                total[last, at, :] = total[last, at, :] + part[last, x, side, tap]
+        add_q(last)
+
+    def last_sum():
+        for step in (1, 3, 2):
+            x_out(step).wait_recv()
+        got = x_got[0] + x_got[1] + x_got[2]
+        filled = jnp.concatenate([got, jnp.zeros((128 - rank, got.shape[1]), jnp.float32)], axis=0).T
+        count = part.shape[4]
+        for side in range(2):
+            for tap in range(TAPS):
+                at = pl.ds(side * count * TAPS + tap, count, stride=TAPS)
+                line = (side * TAPS + tap) * count
+                q_sum[at, :] = q_sum[at, :] + filled[line : line + count]
 
     def multiply(first, count, after):
         depth = gbuf.shape[1]
@@ -458,6 +492,17 @@
         mem_out(k).start()
         pl.when(with_q)(lambda: add_q(k))
 
+    def complete_last():
+        for group in range(3):
+            near(last, 0, group).wait_recv()
+            near(last, 1, group).wait_recv()
+        count = part.shape[4]
+        for side in range(2):
+            for tap in range(TAPS):
+                at = pl.ds(side * count * TAPS + tap, count, stride=TAPS)
+                total[last, at, :] = total[last, at, :] + (piece[last, 0, side, tap] + piece[last, 1, side, tap])
+        mem_out(last).start()
+
     def over(first, count, body):
         def one(i, carry):
             body(first + i)
@@ -492,19 +537,21 @@
             t_finish()
 
         pl.when(j == T_AT + 1)(t_pass_on)
+        pl.when(j == last)(last_terms)
+
         for at, stage in zip(P_AT, (p_terms, p_sum_sp, p_sum_rep, orthogonal)):
             pl.when(j == at)(stage)
         ready = j >= P_AT[-1]
 
-        pl.when((j == 2) | (j == CHUNKS + 1))(lambda: complete(lax.select(j == 2, 0, CHUNKS - 1), ready))
-        pl.when((j > 2) & (j <= CHUNKS) & even)(
-            lambda: over(j - 3, 2, lambda k: complete(k, ready))
-        )
+        pl.when(j == 2)(lambda: complete(0, ready))
+        pl.when((j > 2) & (j <= CHUNKS) & even)(lambda: over(j - 3, 2, lambda k: complete(k, ready)))
         pl.when(j == P_AT[-1])(lambda: over(0, EARLY, add_q))
 
         return carry
 
-    lax.fori_loop(0, CHUNKS + 2, step, 0)
+    lax.fori_loop(0, CHUNKS + 1, step, 0)
+    last_own()
+    last_sum()
 
     lines = rank // count_rep
     q_lines = q_sum[...].T
@@ -519,6 +566,7 @@
     q_next[rep] = acc * (1.0 / count_rep)
     for d in range(1, count_rep):
         q_gather(d).start()
+    complete_last()
     for d in range(1, count_rep):
         q_gather_in(d).wait_recv()
 
@@ -541,6 +589,7 @@
         t_out(side).wait_send()
     for step_ in (1, 3, 2):
         q_out(step_).wait_send()
+        x_out(step_).wait_send()
     for d in range(1, count_sp):
         p_scatter(d).wait_send()
         p_gather(d).wait_send()
@@ -569,7 +618,7 @@
         out_shape=(
             jax.ShapeDtypeStruct((rows, chans), f32),
             jax.ShapeDtypeStruct((count_rep, *q_block), f32),
-            jax.ShapeDtypeStruct((CHUNKS, rank, COLS), f32),
+            jax.ShapeDtypeStruct((6 * rank, chans), bf16),
         ),
         in_specs=[any_spec, any_spec, any_spec, vmem_spec],
         out_specs=(any_spec, vmem_spec, vmem_spec),
@@ -601,12 +650,14 @@
             pltpu.VMEM((count_rep, *q_block), f32),
             pltpu.VMEM((count_rep - 1, *q_block), f32),
             pltpu.VMEM((rows, 128), f32),
+            pltpu.VMEM((RING - 1, rank, rows), f32),
+            pltpu.VMEM((RING - 1, rank, rows), f32),
             dma((chans // COLS,)), dma((6,)), dma((6,)), dma, dma((2,)), dma((2,)), dma((CHUNKS,)), dma((CHUNKS,)),
             two, two, two, two, three, three, three, three, dma((CHUNKS,)),
             dma((3,)), dma((3,)), dma, dma((4,)), dma((4,)),
             dma((count_sp - 1,)), dma((count_sp - 1,)), dma((count_rep - 1,)), dma((count_rep - 1,)),
             dma((count_sp - 1,)), dma((count_sp - 1,)), dma((count_rep - 1,)), dma((count_rep - 1,)),
-            dma((count_rep - 1,)), dma((count_rep - 1,)),
+            dma((count_rep - 1,)), dma((count_rep - 1,)), dma((3,)), dma((3,)),
         ],
         compiler_params=pltpu.CompilerParams(
             collective_id=0, has_side_effects=True, vmem_limit_bytes=58 * 1024 * 1024
@@ -616,8 +667,9 @@
     )(frames, g, err, q_own)
 
 
-def feedback_kernel(memory, q_parts, p_ortho, error_next, q_next, q_side):
+def feedback_kernel(memory, q_parts, p_side, error_next, q_next, q_side):
     count, lines, rows = q_parts.shape
+    block = memory.shape[0]
 
     @pl.when(pl.program_id(0) == 0)
     def _():
@@ -626,46 +678,42 @@
         q0, q1, q2 = split(q_next[...])
         q_side[...] = jnp.concatenate([q0, q0, q0, q1, q1, q2], axis=0).T
 
-    for i in range(p_ortho.shape[0]):
-        p0, p1, p2 = split(p_ortho[i])
-        p_side = jnp.concatenate([p0, p1, p2, p0, p1, p0], axis=0)
-        at = slice(i * COLS, (i + 1) * COLS)
-        error_next[:, at] = memory[:, at] - jnp.dot(q_side[...], p_side, preferred_element_type=jnp.float32)
-
-
-def feedback(memory, q_parts, p_ortho):
+    at = pl.ds(pl.multiple_of(pl.program_id(0) * block, block), block)
+    error_next[...] = memory[...] - jnp.dot(q_side[at, :], p_side[...], preferred_element_type=jnp.float32)
+
+
+def feedback(memory, q_parts, p_side):
     rows, chans = memory.shape
     count, lines, _ = q_parts.shape
     rank = count * lines
-    per_block = 2
-    block = (rows, per_block * COLS)
+    block = (rows // 4, chans)
     return pl.pallas_call(
         feedback_kernel,
-        grid=(chans // block[1],),
+        grid=(rows // block[0],),
         out_shape=(jax.ShapeDtypeStruct(memory.shape, jnp.float32), jax.ShapeDtypeStruct((rank, rows), jnp.float32)),
         in_specs=[
-            pl.BlockSpec(block, lambda i: (0, i)),
+            pl.BlockSpec(block, lambda i: (i, 0)),
             pl.BlockSpec(q_parts.shape, lambda i: (0, 0, 0)),
-            pl.BlockSpec((per_block, rank, COLS), lambda i: (i, 0, 0)),
+            pl.BlockSpec(p_side.shape, lambda i: (0, 0)),
         ],
-        out_specs=(pl.BlockSpec(block, lambda i: (0, i)), pl.BlockSpec((rank, rows), lambda i: (0, 0))),
+        out_specs=(pl.BlockSpec(block, lambda i: (i, 0)), pl.BlockSpec((rank, rows), lambda i: (0, 0))),
         scratch_shapes=[pltpu.VMEM((rows, 6 * rank), jnp.bfloat16)],
         compiler_params=pltpu.CompilerParams(vmem_limit_bytes=60 * 1024 * 1024),
         name="feedback",
-    )(memory, q_parts, p_ortho)
+    )(memory, q_parts, p_side)
 
 
 def per_device(count_rep, frames, out_grad, error_prev, q_prev):
     band_rows, width, chans = frames.shape[1:]
     band = band_rows * width
-    memory, q_parts, p_ortho = compressed_step(
+    memory, q_parts, p_side = compressed_step(
         count_rep,
         frames[0].reshape(band, chans),
         out_grad[0].reshape(band, chans),
         error_prev[0],
         q_prev,
     )
-    error_next, q_next = feedback(memory, q_parts, p_ortho)
+    error_next, q_next = feedback(memory, q_parts, p_side)
     return (error_next[None], q_next)
 
 

time: 160 us -> 160 us (level)
  no operation moved by 1% of the time
where the time goes in v6:
time: 160 us; the launch traced here: 159 us
  Pallas kernels  159 us (99%)
    pallas_call x1, Pallas kernels, compressed_step(): pl.pallas_call(functools.partial(step_kernel, count_rep), out_shape=(jax....  154 us
    pallas_call x1, Pallas kernels, feedback(): pl.pallas_call(feedback_kernel, grid=(rows // block[0],), out_shape=(jax....  4.57 us

profile of v6, /device:TPU:1, one launch (start us, length us, event | category | flops | bytes accessed | tf_op | source)
XLA Modules:
  0.0 159.4 jit_solution(2423548656312196969)
XLA Ops:
  0.6 154.2 %compressed_step.1 = (f32[576,1024]{1,0:T(8,128)}, f32[8,4,576]{2,1,0:T(4,128)}, bf16[192,1024]{1,0:T(8,128)(2,1)}) custom-call(bf16[1024,1024]{1,0:T(8,128)(2,1)} %bitcast.6, bf16[1024,1024]{1,0:T(8,128)(2,1)} %bitcast.7, f32[576,1024]{1,0:T(8,128)} %bitcast.4, f32[32,576]{1,0:T(8,128)} %q_own.1), custom_call_target="tpu_custom_call" | custom-call | flops 19327352832 | bytes 10000000 | tf_op jit(solution)/shard_map/compressed_step/pallas_call | solution.py:616
  154.8 4.6 %feedback.1 = (f32[576,1024]{1,0:T(8,128)}, f32[32,576]{1,0:T(8,128)}) custom-call(f32[576,1024]{1,0:T(8,128)} %get-tuple-element.7.memory, f32[8,4,576]{2,1,0:T(4,128)} %get-tuple-element.8.q_parts, bf16[192,1024]{1,0:T(8,128)(2,1)} %get-tuple-element.9.p_side), custom_call_target="tpu_custom_call" | custom-call | tf_op jit(solution)/shard_map/feedback/pallas_call | solution.py:690

commit v7 on v6

--- a/solution.py
+++ b/solution.py
@@ -44,7 +44,7 @@
 def step_kernel(
     count_rep, frames, g, err, q_own, memory, q_next, p_side,
     local, f_relay, t_relay, q_turned, q_taps, flipped, raw, halo, taps, gbuf, part, relay, piece, total,
-    q_near, q_flip, t_term, t_near, p_src, p_near, p_one, p_far, p_all, work, q_src, q_got, q_sum, x_term, x_got,
+    q_near, q_flip, t_work, t_term, t_near, p_src, p_near, p_one, p_far, p_all, work, q_src, q_got, q_sum, x_term, x_got,
     l_in, f_send, f_recv, f_own, h_send, h_recv, e_in, g_own,
     d_send, d_recv, r_send, r_recv, a_send, a_recv, b_send, b_recv, out_sem,
     q_send, q_recv, q_copy, t_send, t_recv, s1, r1, s2, r2, s3, r3, s4, r4, s5, r5, x_send, x_recv,
@@ -265,19 +265,13 @@
     start_forward(0)
     for j in range(1, CHUNKS):
         own_grad(j).wait()
-
-    for j in range(CHUNKS):
-        err_in(j).wait()
-        term = exact_dot(q_own[...], total[j], ((1,), (0,)))
-        for h in range(2):
-            p_src[2 * j + h] = term[h * (rank // 2) : (h + 1) * (rank // 2)]
+    start_direct(1)
 
     for side in range(2):
         frames_far(side).wait_recv()
         frames_on(side).start()
     for side in range(2):
         frames_near_in(side).wait_recv()
-    start_direct(1)
     place_band(z_down)
     place_band(z_up)
     for side in range(2):
@@ -296,28 +290,56 @@
     place(0, jnp.where(x == 0, zero, halo[0].reshape(RING * share, width)))
     place(rows + 1, jnp.where(x == RING - 1, zero, halo[1].reshape(RING * share, width)))
 
-    def t_band(which):
-        acc = None
-        for a in range(3):
-            at = pl.ds(pl.multiple_of(which * band + a * width, width), band)
-            stacked = taps[:, :, at].reshape(3 * RING * share, band)
-            term = jnp.dot(q_flip[a], stacked, preferred_element_type=jnp.float32)
-            acc = term if acc is None else acc + term
-        t_term[which] = acc[:rank] + (acc[rank : 2 * rank] + acc[2 * rank : 3 * rank])
-
     def t_start():
         own_q.wait()
         for step in (1, 3, 2):
             q_in(step).wait_recv()
-        for a in range(3):
-            q_flip[a] = q_near[3 * a : 3 * a + 3].reshape(3 * RING * share, lanes).T
-
-    def t_bands(first):
-        def one(i, carry):
-            t_band(first + i)
+        for tap in range(TAPS):
+            turned = q_near[tap].reshape(RING * share, lanes).T
+            q_flip[tap * 3 * rank : (tap + 1) * 3 * rank] = turned[: 3 * rank]
+        t_work[...] = jnp.zeros_like(t_work)
+
+    def t_rows():
+        def one(row, carry):
+            at = pl.ds(pl.multiple_of(row * width, width), width)
+            product = jnp.dot(q_flip[...], taps[1, :, at], preferred_element_type=jnp.float32)
+            for a in range(3):
+                for b in range(3):
+                    line = (a * 3 + b) * 3 * rank
+                    term = product[line : line + rank] + (
+                        product[line + rank : line + 2 * rank] + product[line + 2 * rank : line + 3 * rank]
+                    )
+                    t_work[b, row + 2 - a] = t_work[b, row + 2 - a] + term
             return carry
 
-        lax.fori_loop(0, RING // 2, one, 0)
+        lax.fori_loop(0, rows + 2, one, 0)
+        lane_of = lax.broadcasted_iota(jnp.int32, (rank, width), 1)
+        per_band = band // width
+        for row in range(rows):
+            before = jnp.where(lane_of == 0, 0.0, pltpu.roll(t_work[0, row + 2], 1, 1))
+            after = jnp.where(lane_of == width - 1, 0.0, pltpu.roll(t_work[2, row + 2], width - 1, 1))
+            spot = (row % per_band) * width
+            t_term[row // per_band, :, spot : spot + width] = t_work[1, row + 2] + (before + after)
+
+    def p_start():
+        for j in range(CHUNKS):
+            err_in(j).wait()
+        q0, q1, _ = split(q_own[...])
+        both = jnp.concatenate([q0, q1], axis=0)
+
+        def two(i, carry):
+            j = 2 * i
+            e0, e1, _ = split(jnp.concatenate([total[j], total[j + 1]], axis=1))
+            main = jnp.dot(both, e0, preferred_element_type=jnp.float32)
+            term = main[:rank] + (main[rank:] + jnp.dot(q0, e1, preferred_element_type=jnp.float32))
+            for c in range(2):
+                for h in range(2):
+                    p_src[2 * (j + c) + h] = term[
+                        h * (rank // 2) : (h + 1) * (rank // 2), c * COLS : (c + 1) * COLS
+                    ]
+            return carry
+
+        lax.fori_loop(0, CHUNKS // 2, two, 0)
 
     def t_finish():
         for side in range(2):
@@ -532,11 +554,13 @@
         @pl.when(j == T_AT)
         def _():
             t_start()
-            t_bands(0)
-            t_bands(RING // 2)
+            t_rows()
             t_finish()
 
-        pl.when(j == T_AT + 1)(t_pass_on)
+        @pl.when(j == T_AT + 1)
+        def _():
+            t_pass_on()
+            p_start()
         pl.when(j == last)(last_terms)
 
         for at, stage in zip(P_AT, (p_terms, p_sum_sp, p_sum_rep, orthogonal)):
@@ -638,7 +662,8 @@
             pltpu.VMEM((CHUNKS, 2, 2, TAPS, per_side, COLS), f32),
             pltpu.VMEM((CHUNKS, rows, COLS), f32),
             pltpu.VMEM((TAPS, RING, share, 128), bf16),
-            pltpu.VMEM((3, 128, 3 * RING * share), bf16),
+            pltpu.VMEM((TAPS * 3 * rank, RING * share), bf16),
+            pltpu.VMEM((3, RING * band // width + 4, rank, width), f32),
             pltpu.VMEM((RING, rank, band), f32),
             pltpu.VMEM((2, rank, band), f32),
             pltpu.VMEM((count_sp, *p_block), f32),

time: 160 us -> 167 us (1.044)
  Pallas kernels: 159 us -> 167 us
    pallas_call x1, Pallas kernels: 154 us -> 162 us  [compressed_step(): pl.pallas_call(functools.partial(step_kernel, count_rep), out_shape=(jax....]
where the time goes in v7:
time: 167 us
  Pallas kernels  167 us (100%)
    pallas_call x1, Pallas kernels, compressed_step(): pl.pallas_call(functools.partial(step_kernel, count_rep), out_shape=(jax....  162 us
    pallas_call x1, Pallas kernels, feedback(): pl.pallas_call(feedback_kernel, grid=(rows // block[0],), out_shape=(jax....  4.57 us

profile of v7, /device:TPU:1, one launch (start us, length us, event | category | flops | bytes accessed | tf_op | source)
XLA Modules:
  0.0 167.2 jit_solution(666219733268350954)
XLA Ops:
  0.6 162.0 %compressed_step.1 = (f32[576,1024]{1,0:T(8,128)}, f32[8,4,576]{2,1,0:T(4,128)}, bf16[192,1024]{1,0:T(8,128)(2,1)}) custom-call(bf16[1024,1024]{1,0:T(8,128)(2,1)} %bitcast.6, bf16[1024,1024]{1,0:T(8,128)(2,1)} %bitcast.7, f32[576,1024]{1,0:T(8,128)} %bitcast.4, f32[32,576]{1,0:T(8,128)} %q_own.1), custom_call_target="tpu_custom_call" | custom-call | flops 19327352832 | bytes 10000000 | tf_op jit(solution)/shard_map/compressed_step/pallas_call | solution.py:640
  162.6 4.6 %feedback.1 = (f32[576,1024]{1,0:T(8,128)}, f32[32,576]{1,0:T(8,128)}) custom-call(f32[576,1024]{1,0:T(8,128)} %get-tuple-element.7.memory, f32[8,4,576]{2,1,0:T(4,128)} %get-tuple-element.8.q_parts, bf16[192,1024]{1,0:T(8,128)(2,1)} %get-tuple-element.9.p_side), custom_call_target="tpu_custom_call" | custom-call | tf_op jit(solution)/shard_map/feedback/pallas_call | solution.py:715

commit v8 on v6

--- a/solution.py
+++ b/solution.py
@@ -125,18 +125,16 @@
     def mem_out(j):
         return pltpu.make_async_copy(total.at[j], memory.at[:, columns(j)], out_sem.at[j])
 
-    def far(j, side, group):
-        some = pl.ds(group * 3, 3)
+    def far(j, side):
         return remote(
-            part.at[j, x_far, side, some], relay.at[j, side, some], a_send.at[j, side, group],
-            a_recv.at[j, side, group], right if side == 0 else left,
+            part.at[j, x_far, side], relay.at[j, side], a_send.at[j, side], a_recv.at[j, side],
+            right if side == 0 else left,
         )
 
-    def near(j, side, group):
-        some = pl.ds(group * 3, 3)
+    def near(j, side):
         return remote(
-            part.at[j, x_right if side == 0 else x_left, :, some], piece.at[j, side, :, some],
-            b_send.at[j, side, group], b_recv.at[j, side, group], right if side == 0 else left,
+            part.at[j, x_right if side == 0 else x_left], piece.at[j, side], b_send.at[j, side], b_recv.at[j, side],
+            right if side == 0 else left,
         )
 
     def q_out(step):
@@ -457,9 +455,6 @@
                             part[first + c, owner, side, a * 3 + b] = product[
                                 line : line + per_side, c * COLS : (c + 1) * COLS
                             ]
-                far(first + c, 0, a).start()
-                far(first + c, 1, a).start()
-
             @pl.when((a == 0) & (after < CHUNKS))
             def _():
                 start_forward(after)
@@ -467,21 +462,21 @@
             return carry
 
         lax.fori_loop(0, 3, one, 0)
+        for c in range(count):
+            far(first + c, 0).start()
+            far(first + c, 1).start()
 
     def pass_on(k):
-        for group in range(3):
-            some = pl.ds(group * 3, 3)
-            far(k, 0, group).wait_recv()
-            part[k, x_right, 0, some] = part[k, x_right, 0, some] + relay[k, 0, some]
-            near(k, 0, group).start()
-            far(k, 1, group).wait_recv()
-            part[k, x_left, 1, some] = part[k, x_left, 1, some] + relay[k, 1, some]
-            near(k, 1, group).start()
+        far(k, 0).wait_recv()
+        part[k, x_right, 0] = part[k, x_right, 0] + relay[k, 0]
+        near(k, 0).start()
+        far(k, 1).wait_recv()
+        part[k, x_left, 1] = part[k, x_left, 1] + relay[k, 1]
+        near(k, 1).start()
 
     def complete(k, with_q):
-        for group in range(3):
-            near(k, 0, group).wait_recv()
-            near(k, 1, group).wait_recv()
+        near(k, 0).wait_recv()
+        near(k, 1).wait_recv()
         count = part.shape[4]
         for side in range(2):
             for tap in range(TAPS):
@@ -493,9 +488,8 @@
         pl.when(with_q)(lambda: add_q(k))
 
     def complete_last():
-        for group in range(3):
-            near(last, 0, group).wait_recv()
-            near(last, 1, group).wait_recv()
+        near(last, 0).wait_recv()
+        near(last, 1).wait_recv()
         count = part.shape[4]
         for side in range(2):
             for tap in range(TAPS):
@@ -574,9 +568,8 @@
         for side in range(2):
             direct(j, side).wait_send()
             forward(j, side).wait_send()
-            for group in range(3):
-                far(j, side, group).wait_send()
-                near(j, side, group).wait_send()
+            far(j, side).wait_send()
+            near(j, side).wait_send()
         mem_out(j).wait()
         return carry
 
@@ -608,7 +601,7 @@
     share = chans // count_sp
     per_side = share // 2
     dma = pltpu.SemaphoreType.DMA
-    two, three = dma((CHUNKS, 2)), dma((CHUNKS, 2, 3))
+    two = dma((CHUNKS, 2))
     f32, bf16 = jnp.float32, jnp.bfloat16
     any_spec, vmem_spec = pl.BlockSpec(memory_space=pl.ANY), pl.BlockSpec(memory_space=pltpu.VMEM)
     p_block = (rank // 2, COLS)
@@ -653,7 +646,7 @@
             pltpu.VMEM((RING - 1, rank, rows), f32),
             pltpu.VMEM((RING - 1, rank, rows), f32),
             dma((chans // COLS,)), dma((6,)), dma((6,)), dma, dma((2,)), dma((2,)), dma((CHUNKS,)), dma((CHUNKS,)),
-            two, two, two, two, three, three, three, three, dma((CHUNKS,)),
+            two, two, two, two, two, two, two, two, dma((CHUNKS,)),
             dma((3,)), dma((3,)), dma, dma((4,)), dma((4,)),
             dma((count_sp - 1,)), dma((count_sp - 1,)), dma((count_rep - 1,)), dma((count_rep - 1,)),
             dma((count_sp - 1,)), dma((count_sp - 1,)), dma((count_rep - 1,)), dma((count_rep - 1,)),

time: 160 us -> 162 us (1.012)
  Pallas kernels: 159 us -> 161 us
    pallas_call x1, Pallas kernels: 154 us -> 156 us  [compressed_step(): pl.pallas_call(functools.partial(step_kernel, count_rep), out_shape=(jax....]
where the time goes in v8:
time: 162 us; the launch traced here: 161 us
  Pallas kernels  161 us (99%)
    pallas_call x1, Pallas kernels, compressed_step(): pl.pallas_call(functools.partial(step_kernel, count_rep), out_shape=(jax....  156 us
    pallas_call x1, Pallas kernels, feedback(): pl.pallas_call(feedback_kernel, grid=(rows // block[0],), out_shape=(jax....  4.57 us

profile of v8, /device:TPU:1, one launch (start us, length us, event | category | flops | bytes accessed | tf_op | source)
XLA Modules:
  0.0 161.4 jit_solution(18068089178338197645)
XLA Ops:
  0.6 156.2 %compressed_step.1 = (f32[576,1024]{1,0:T(8,128)}, f32[8,4,576]{2,1,0:T(4,128)}, bf16[192,1024]{1,0:T(8,128)(2,1)}) custom-call(bf16[1024,1024]{1,0:T(8,128)(2,1)} %bitcast.6, bf16[1024,1024]{1,0:T(8,128)(2,1)} %bitcast.7, f32[576,1024]{1,0:T(8,128)} %bitcast.4, f32[32,576]{1,0:T(8,128)} %q_own.1), custom_call_target="tpu_custom_call" | custom-call | flops 19327352832 | bytes 10000000 | tf_op jit(solution)/shard_map/compressed_step/pallas_call | solution.py:609
  156.8 4.6 %feedback.1 = (f32[576,1024]{1,0:T(8,128)}, f32[32,576]{1,0:T(8,128)}) custom-call(f32[576,1024]{1,0:T(8,128)} %get-tuple-element.7.memory, f32[8,4,576]{2,1,0:T(4,128)} %get-tuple-element.8.q_parts, bf16[192,1024]{1,0:T(8,128)(2,1)} %get-tuple-element.9.p_side), custom_call_target="tpu_custom_call" | custom-call | tf_op jit(solution)/shard_map/feedback/pallas_call | solution.py:683

commit v9 on v8

--- a/solution.py
+++ b/solution.py
@@ -41,9 +41,34 @@
     )
 
 
+SCALE_ROWS = 16
+RANGE = 1024.0
+
+
+def encode(block):
+    largest = jnp.max(jnp.abs(block), axis=(0, 1), keepdims=True)
+    scale = jnp.maximum(largest * 1.01, 1e-30).astype(jnp.bfloat16)
+    size = jnp.abs(block) * (RANGE / scale.astype(jnp.float32))
+    second = size * size
+    fourth = second * second
+    twelfth = fourth * fourth * fourth
+    signed = jnp.where(block < 0, -twelfth, twelfth).astype(jnp.bfloat16)
+    return signed, jnp.broadcast_to(scale, (SCALE_ROWS, block.shape[1]))
+
+
+def decode(coded):
+    count = coded.shape[0] - SCALE_ROWS
+    signed = coded[:count].astype(jnp.float32)
+    scale = coded[count : count + 1].astype(jnp.float32) * (1.0 / RANGE)
+    size = jnp.abs(signed)
+    value = jnp.exp(jnp.log(jnp.maximum(size, 1e-37)) * (1.0 / 12.0)) * scale
+    value = jnp.where(size < 1e-37, 0.0, value)
+    return jnp.where(signed < 0, -value, value)
+
+
 def step_kernel(
     count_rep, frames, g, err, q_own, memory, q_next, p_side,
-    local, f_relay, t_relay, q_turned, q_taps, flipped, raw, halo, taps, gbuf, part, relay, piece, total,
+    local, f_relay, t_relay, q_turned, q_taps, flipped, raw, halo, taps, gbuf, part, far_code, near_code, relay, piece, total,
     q_near, q_flip, t_term, t_near, p_src, p_near, p_one, p_far, p_all, work, q_src, q_got, q_sum, x_term, x_got,
     l_in, f_send, f_recv, f_own, h_send, h_recv, e_in, g_own,
     d_send, d_recv, r_send, r_recv, a_send, a_recv, b_send, b_recv, out_sem,
@@ -127,13 +152,13 @@
 
     def far(j, side):
         return remote(
-            part.at[j, x_far, side], relay.at[j, side], a_send.at[j, side], a_recv.at[j, side],
+            far_code.at[j, side], relay.at[j, side], a_send.at[j, side], a_recv.at[j, side],
             right if side == 0 else left,
         )
 
     def near(j, side):
         return remote(
-            part.at[j, x_right if side == 0 else x_left], piece.at[j, side], b_send.at[j, side], b_recv.at[j, side],
+            near_code.at[j, side], piece.at[j, side], b_send.at[j, side], b_recv.at[j, side],
             right if side == 0 else left,
         )
 
@@ -463,38 +488,47 @@
 
         lax.fori_loop(0, 3, one, 0)
         for c in range(count):
-            far(first + c, 0).start()
-            far(first + c, 1).start()
+            for side in range(2):
+                put(far_code.at[first + c, side], part[first + c, x_far, side].reshape(half_rows, COLS))
+                far(first + c, side).start()
+
+    half_rows = TAPS * part.shape[4]
+
+    def put(ref, block):
+        signed, scale = encode(block)
+        ref[:half_rows] = signed
+        ref[half_rows:] = scale
 
     def pass_on(k):
-        far(k, 0).wait_recv()
-        part[k, x_right, 0] = part[k, x_right, 0] + relay[k, 0]
-        near(k, 0).start()
-        far(k, 1).wait_recv()
-        part[k, x_left, 1] = part[k, x_left, 1] + relay[k, 1]
-        near(k, 1).start()
+        for side, owner in ((0, x_right), (1, x_left)):
+            put(near_code.at[k, side, 1 - side], part[k, owner, 1 - side].reshape(half_rows, COLS))
+            far(k, side).wait_recv()
+            both = part[k, owner, side].reshape(half_rows, COLS) + decode(relay[k, side])
+            put(near_code.at[k, side, side], both)
+            near(k, side).start()
+
+    def add_near(k, own):
+        count = part.shape[4]
+        for side in range(2):
+            got = decode(piece[k, 0, side]) + decode(piece[k, 1, side])
+            for tap in range(TAPS):
+                at = pl.ds(side * count * TAPS + tap, count, stride=TAPS)
+                term = got[tap * count : (tap + 1) * count]
+                if own:
+                    term = term + part[k, x, side, tap]
+                total[k, at, :] = total[k, at, :] + term
 
     def complete(k, with_q):
         near(k, 0).wait_recv()
         near(k, 1).wait_recv()
-        count = part.shape[4]
-        for side in range(2):
-            for tap in range(TAPS):
-                at = pl.ds(side * count * TAPS + tap, count, stride=TAPS)
-                total[k, at, :] = (
-                    total[k, at, :] + part[k, x, side, tap] + (piece[k, 0, side, tap] + piece[k, 1, side, tap])
-                )
+        add_near(k, True)
         mem_out(k).start()
         pl.when(with_q)(lambda: add_q(k))
 
     def complete_last():
         near(last, 0).wait_recv()
         near(last, 1).wait_recv()
-        count = part.shape[4]
-        for side in range(2):
-            for tap in range(TAPS):
-                at = pl.ds(side * count * TAPS + tap, count, stride=TAPS)
-                total[last, at, :] = total[last, at, :] + (piece[last, 0, side, tap] + piece[last, 1, side, tap])
+        add_near(last, False)
         mem_out(last).start()
 
     def over(first, count, body):
@@ -600,6 +634,7 @@
     count_sp = RING * RING
     share = chans // count_sp
     per_side = share // 2
+    code_rows = TAPS * per_side + SCALE_ROWS
     dma = pltpu.SemaphoreType.DMA
     two = dma((CHUNKS, 2))
     f32, bf16 = jnp.float32, jnp.bfloat16
@@ -627,8 +662,10 @@
             pltpu.VMEM((3, RING * share, RING * band + 2 * width), bf16),
             pltpu.VMEM((CHUNKS, RING * band, COLS), bf16),
             pltpu.VMEM((CHUNKS, RING, 2, TAPS, per_side, COLS), f32),
-            pltpu.VMEM((CHUNKS, 2, TAPS, per_side, COLS), f32),
-            pltpu.VMEM((CHUNKS, 2, 2, TAPS, per_side, COLS), f32),
+            pltpu.VMEM((CHUNKS, 2, code_rows, COLS), bf16),
+            pltpu.VMEM((CHUNKS, 2, 2, code_rows, COLS), bf16),
+            pltpu.VMEM((CHUNKS, 2, code_rows, COLS), bf16),
+            pltpu.VMEM((CHUNKS, 2, 2, code_rows, COLS), bf16),
             pltpu.VMEM((CHUNKS, rows, COLS), f32),
             pltpu.VMEM((TAPS, RING, share, 128), bf16),
             pltpu.VMEM((3, 128, 3 * RING * share), bf16),

time: 162 us -> 151 us (0.932)
  Pallas kernels: 161 us -> 150 us
    pallas_call x1, Pallas kernels: 156 us -> 146 us  [compressed_step(): pl.pallas_call(functools.partial(step_kernel, count_rep), out_shape=(jax....]
where the time goes in v9:
time: 151 us
  Pallas kernels  150 us (99%)
    pallas_call x1, Pallas kernels, compressed_step(): pl.pallas_call(functools.partial(step_kernel, count_rep), out_shape=(jax....  146 us
    pallas_call x1, Pallas kernels, feedback(): pl.pallas_call(feedback_kernel, grid=(rows // block[0],), out_shape=(jax....  4.58 us

profile of v9, /device:TPU:1, one launch (start us, length us, event | category | flops | bytes accessed | tf_op | source)
XLA Modules:
  0.0 151.0 jit_solution(6929591824549386315)
XLA Ops:
  0.6 145.8 %compressed_step.1 = (f32[576,1024]{1,0:T(8,128)}, f32[8,4,576]{2,1,0:T(4,128)}, bf16[192,1024]{1,0:T(8,128)(2,1)}) custom-call(bf16[1024,1024]{1,0:T(8,128)(2,1)} %bitcast.6, bf16[1024,1024]{1,0:T(8,128)(2,1)} %bitcast.7, f32[576,1024]{1,0:T(8,128)} %bitcast.4, f32[32,576]{1,0:T(8,128)} %q_own.1), custom_call_target="tpu_custom_call" | custom-call | flops 19327352832 | bytes 10000000 | tf_op jit(solution)/shard_map/compressed_step/pallas_call | solution.py:644
  146.4 4.6 %feedback.1 = (f32[576,1024]{1,0:T(8,128)}, f32[32,576]{1,0:T(8,128)}) custom-call(f32[576,1024]{1,0:T(8,128)} %get-tuple-element.7.memory, f32[8,4,576]{2,1,0:T(4,128)} %get-tuple-element.8.q_parts, bf16[192,1024]{1,0:T(8,128)(2,1)} %get-tuple-element.9.p_side), custom_call_target="tpu_custom_call" | custom-call | tf_op jit(solution)/shard_map/feedback/pallas_call | solution.py:720

commit v10 on v9

--- a/solution.py
+++ b/solution.py
@@ -463,7 +463,7 @@
                 line = (side * TAPS + tap) * count
                 q_sum[at, :] = q_sum[at, :] + filled[line : line + count]
 
-    def multiply(first, count, after):
+    def multiply(first, count):
         depth = gbuf.shape[1]
         per_side = part.shape[4]
 
@@ -480,9 +480,10 @@
                             part[first + c, owner, side, a * 3 + b] = product[
                                 line : line + per_side, c * COLS : (c + 1) * COLS
                             ]
-            @pl.when((a == 0) & (after < CHUNKS))
+            @pl.when((a == 0) & (first == 0))
             def _():
-                start_forward(after)
+                start_forward(1)
+                start_direct(3)
 
             return carry
 
@@ -539,9 +540,15 @@
         lax.fori_loop(0, count, one, 0)
 
     def step(j, carry):
-        @pl.when(j + 2 < CHUNKS)
+        pl.when(j == 0)(lambda: start_direct(2))
+
+        @pl.when((j > 0) & (j + 3 < CHUNKS))
         def _():
-            start_direct(j + 2)
+            start_direct(j + 3)
+
+        @pl.when((j > 0) & (j + 2 < CHUNKS))
+        def _():
+            start_forward(j + 2)
 
         @pl.when(j < CHUNKS)
         def _():
@@ -550,9 +557,8 @@
 
         alone = (j == 0) | (j == CHUNKS - 1)
         even = lax.rem(j, 2) == 0
-        pl.when(alone)(lambda: multiply(j, 1, j + 1))
-        pl.when((j > 0) & (j < CHUNKS - 1) & even)(lambda: multiply(j - 1, 2, j + 1))
-        pl.when((j < CHUNKS - 1) & jnp.logical_not(even))(lambda: start_forward(j + 1))
+        pl.when(alone)(lambda: multiply(j, 1))
+        pl.when((j > 0) & (j < CHUNKS - 1) & even)(lambda: multiply(j - 1, 2))
 
         pl.when((j == 1) | (j == CHUNKS))(lambda: pass_on(j - 1))
         pl.when((j > 1) & (j < CHUNKS) & jnp.logical_not(even))(lambda: over(j - 2, 2, pass_on))
@@ -561,6 +567,7 @@
         def _():
             t_start()
             t_bands(0)
+            start_forward(2)
             t_bands(RING // 2)
             t_finish()
 

time: 151 us -> 156 us (1.033)
  Pallas kernels: 150 us -> 155 us
    pallas_call x1, Pallas kernels: 146 us -> 150 us  [compressed_step(): pl.pallas_call(functools.partial(step_kernel, count_rep), out_shape=(jax....]
where the time goes in v10:
time: 156 us
  Pallas kernels  155 us (99%)
    pallas_call x1, Pallas kernels, compressed_step(): pl.pallas_call(functools.partial(step_kernel, count_rep), out_shape=(jax....  150 us
    pallas_call x1, Pallas kernels, feedback(): pl.pallas_call(feedback_kernel, grid=(rows // block[0],), out_shape=(jax....  4.57 us

profile of v10, /device:TPU:1, one launch (start us, length us, event | category | flops | bytes accessed | tf_op | source)
XLA Modules:
  0.0 155.7 jit_solution(18281110810816596080)
XLA Ops:
  0.6 150.5 %compressed_step.1 = (f32[576,1024]{1,0:T(8,128)}, f32[8,4,576]{2,1,0:T(4,128)}, bf16[192,1024]{1,0:T(8,128)(2,1)}) custom-call(bf16[1024,1024]{1,0:T(8,128)(2,1)} %bitcast.6, bf16[1024,1024]{1,0:T(8,128)(2,1)} %bitcast.7, f32[576,1024]{1,0:T(8,128)} %bitcast.4, f32[32,576]{1,0:T(8,128)} %q_own.1), custom_call_target="tpu_custom_call" | custom-call | flops 19327352832 | bytes 10000000 | tf_op jit(solution)/shard_map/compressed_step/pallas_call | solution.py:651
  151.1 4.6 %feedback.1 = (f32[576,1024]{1,0:T(8,128)}, f32[32,576]{1,0:T(8,128)}) custom-call(f32[576,1024]{1,0:T(8,128)} %get-tuple-element.7.memory, f32[8,4,576]{2,1,0:T(4,128)} %get-tuple-element.8.q_parts, bf16[192,1024]{1,0:T(8,128)(2,1)} %get-tuple-element.9.p_side), custom_call_target="tpu_custom_call" | custom-call | tf_op jit(solution)/shard_map/feedback/pallas_call | solution.py:727

commit v11 on v9

--- a/solution.py
+++ b/solution.py
@@ -484,6 +484,10 @@
             def _():
                 start_forward(after)
 
+            @pl.when((a == 0) & (after + 1 < CHUNKS))
+            def _():
+                start_direct(after + 1)
+
             return carry
 
         lax.fori_loop(0, 3, one, 0)
@@ -539,10 +543,6 @@
         lax.fori_loop(0, count, one, 0)
 
     def step(j, carry):
-        @pl.when(j + 2 < CHUNKS)
-        def _():
-            start_direct(j + 2)
-
         @pl.when(j < CHUNKS)
         def _():
             forward_in(j, 0).wait_recv()
@@ -552,7 +552,12 @@
         even = lax.rem(j, 2) == 0
         pl.when(alone)(lambda: multiply(j, 1, j + 1))
         pl.when((j > 0) & (j < CHUNKS - 1) & even)(lambda: multiply(j - 1, 2, j + 1))
-        pl.when((j < CHUNKS - 1) & jnp.logical_not(even))(lambda: start_forward(j + 1))
+
+        @pl.when((j < CHUNKS - 1) & jnp.logical_not(even))
+        def _():
+            start_forward(j + 1)
+            pl.when(j + 2 < CHUNKS)(lambda: start_direct(j + 2))
+
 
         pl.when((j == 1) | (j == CHUNKS))(lambda: pass_on(j - 1))
         pl.when((j > 1) & (j < CHUNKS) & jnp.logical_not(even))(lambda: over(j - 2, 2, pass_on))

time: 151 us -> 150 us (level)
  no operation moved by 1% of the time
where the time goes in v11:
time: 150 us
  Pallas kernels  150 us (100%)
    pallas_call x1, Pallas kernels, compressed_step(): pl.pallas_call(functools.partial(step_kernel, count_rep), out_shape=(jax....  145 us
    pallas_call x1, Pallas kernels, feedback(): pl.pallas_call(feedback_kernel, grid=(rows // block[0],), out_shape=(jax....  4.57 us

profile of v11, /device:TPU:1, one launch (start us, length us, event | category | flops | bytes accessed | tf_op | source)
XLA Modules:
  0.0 150.2 jit_solution(447648878552843883)
XLA Ops:
  0.6 145.0 %compressed_step.1 = (f32[576,1024]{1,0:T(8,128)}, f32[8,4,576]{2,1,0:T(4,128)}, bf16[192,1024]{1,0:T(8,128)(2,1)}) custom-call(bf16[1024,1024]{1,0:T(8,128)(2,1)} %bitcast.6, bf16[1024,1024]{1,0:T(8,128)(2,1)} %bitcast.7, f32[576,1024]{1,0:T(8,128)} %bitcast.4, f32[32,576]{1,0:T(8,128)} %q_own.1), custom_call_target="tpu_custom_call" | custom-call | flops 19327352832 | bytes 10000000 | tf_op jit(solution)/shard_map/compressed_step/pallas_call | solution.py:649
  145.7 4.6 %feedback.1 = (f32[576,1024]{1,0:T(8,128)}, f32[32,576]{1,0:T(8,128)}) custom-call(f32[576,1024]{1,0:T(8,128)} %get-tuple-element.7.memory, f32[8,4,576]{2,1,0:T(4,128)} %get-tuple-element.8.q_parts, bf16[192,1024]{1,0:T(8,128)(2,1)} %get-tuple-element.9.p_side), custom_call_target="tpu_custom_call" | custom-call | tf_op jit(solution)/shard_map/feedback/pallas_call | solution.py:725

commit v12 on v11

--- a/solution.py
+++ b/solution.py
@@ -289,15 +289,27 @@
     for j in range(1, CHUNKS):
         own_grad(j).wait()
 
-    for j in range(CHUNKS):
-        err_in(j).wait()
-        term = exact_dot(q_own[...], total[j], ((1,), (0,)))
-        for h in range(2):
-            p_src[2 * j + h] = term[h * (rank // 2) : (h + 1) * (rank // 2)]
-
     for side in range(2):
         frames_far(side).wait_recv()
         frames_on(side).start()
+
+    for j in range(CHUNKS):
+        err_in(j).wait()
+    q0, q1, _ = split(q_own[...])
+    both = jnp.concatenate([q0, q1], axis=0)
+
+    def p_start(i, carry):
+        j = 2 * i
+        e0, e1, _ = split(jnp.concatenate([total[j], total[j + 1]], axis=1))
+        main = jnp.dot(both, e0, preferred_element_type=jnp.float32)
+        term = main[:rank] + (main[rank:] + jnp.dot(q0, e1, preferred_element_type=jnp.float32))
+        for c in range(2):
+            for h in range(2):
+                p_src[2 * (j + c) + h] = term[h * (rank // 2) : (h + 1) * (rank // 2), c * COLS : (c + 1) * COLS]
+        return carry
+
+    lax.fori_loop(0, CHUNKS // 2, p_start, 0)
+
     for side in range(2):
         frames_near_in(side).wait_recv()
     start_direct(1)

time: 150 us -> 150 us (level)
  no operation moved by 1% of the time
where the time goes in v12:
time: 150 us
  Pallas kernels  150 us (100%)
    pallas_call x1, Pallas kernels, compressed_step(): pl.pallas_call(functools.partial(step_kernel, count_rep), out_shape=(jax....  145 us
    pallas_call x1, Pallas kernels, feedback(): pl.pallas_call(feedback_kernel, grid=(rows // block[0],), out_shape=(jax....  4.57 us

profile of v12, /device:TPU:1, one launch (start us, length us, event | category | flops | bytes accessed | tf_op | source)
XLA Modules:
  0.0 150.2 jit_solution(5198881844884536815)
XLA Ops:
  0.6 145.0 %compressed_step.1 = (f32[576,1024]{1,0:T(8,128)}, f32[8,4,576]{2,1,0:T(4,128)}, bf16[192,1024]{1,0:T(8,128)(2,1)}) custom-call(bf16[1024,1024]{1,0:T(8,128)(2,1)} %bitcast.6, bf16[1024,1024]{1,0:T(8,128)(2,1)} %bitcast.7, f32[576,1024]{1,0:T(8,128)} %bitcast.4, f32[32,576]{1,0:T(8,128)} %q_own.1), custom_call_target="tpu_custom_call" | custom-call | flops 19327352832 | bytes 10000000 | tf_op jit(solution)/shard_map/compressed_step/pallas_call | solution.py:661
  145.7 4.6 %feedback.1 = (f32[576,1024]{1,0:T(8,128)}, f32[32,576]{1,0:T(8,128)}) custom-call(f32[576,1024]{1,0:T(8,128)} %get-tuple-element.7.memory, f32[8,4,576]{2,1,0:T(4,128)} %get-tuple-element.8.q_parts, bf16[192,1024]{1,0:T(8,128)(2,1)} %get-tuple-element.9.p_side), custom_call_target="tpu_custom_call" | custom-call | tf_op jit(solution)/shard_map/feedback/pallas_call | solution.py:737
